TPU v7x, 128 devices: a whole 4x4x4 slice. The times are simulated.
128 devices in a mesh: seq: 32 (over y, z, x_hi), head: 4 (over x_lo, core).
Axes of the slice: x: 4 (x_hi: 2, x_lo: 2; x = x_hi * 2 + x_lo), y: 4, z: 4, core: 2. Of those that a mesh axis runs over, the one named last changes fastest.
Arguments:
- query: bfloat16 [12288, 1024], P('seq', 'head'), may hold values from -6 to 6
- key: bfloat16 [12288, 1024], P('seq', 'head'), may hold values from -6 to 6
- value: bfloat16 [12288, 1024], P('seq', 'head'), may hold values from -6 to 6
- attn_out: bfloat16 [12288, 1024], P('seq', 'head'), may hold values from -4 to 4
- log_norm: float32 [16, 12288], P('head', 'seq')
- d_output: bfloat16 [12288, 1024], P('seq', 'head'), may hold values from -2 to 2
- out_weight: bfloat16 [1024, 1024], P('head'), may hold values from -0.1875 to 0.1875
- coords: bfloat16 [3, 12288], P(None, 'seq'), may hold values from -5 to 5
- slopes: float32 [16], P('head'), may hold values from 0.05 to 2, as said below
Outputs:
- d_query: bfloat16 [12288, 1024], P('seq', 'head')
- d_key: bfloat16 [12288, 1024], P('seq', 'head')
- d_value: bfloat16 [12288, 1024], P('seq', 'head')
- d_out_weight: float32 [1024, 1024], P('head')
- d_slopes: float32 [16], P('head')
Inputs may be any that keep to these rules, and one draw needn't show every extreme that they name: slopes: one rate a head.
All inputs are finite; a program needn't handle non-finite values.
Results may differ from a plain program's by a relative error of at most 0.023.
Values may be sent and summed in bfloat16 or wider, within the bound.
A program may use at most 64 MiB of HBM per device.

v0:
```python
import jax
import jax.numpy as jnp
from jax import lax
from jax.sharding import PartitionSpec as P

HEAD_DIM = 64


def from_behind(block, axis, distance):
    devices = range(lax.axis_size(axis))
    route = [((i - distance) % len(devices), i) for i in devices]
    return lax.ppermute(block, axis, route)


def distance(mine, theirs):
    total = jnp.ones((mine.shape[1], theirs.shape[1]), jnp.float32)
    for component in range(3):
        offset = (
            mine[component].astype(jnp.float32)[:, None]
            - theirs[component].astype(jnp.float32)[None, :]
        )
        total = total + offset * offset
    return jnp.sqrt(total)


def attend(
    query_heads, dout_heads, row_delta, norm_rows, rates, key_blk, val_blk, query_pos, key_pos
):
    scale = HEAD_DIM ** (-0.5)
    lengths = distance(query_pos, key_pos)
    scores = jnp.einsum("ihd,jhd->hij", query_heads, key_blk, preferred_element_type=jnp.float32)
    attn_probs = jnp.exp(
        scores * scale - rates[:, None, None] * lengths[None] - norm_rows[:, :, None]
    )
    probs_b = attn_probs.astype(jnp.bfloat16)
    value_add = jnp.einsum("hij,ihd->jhd", probs_b, dout_heads, preferred_element_type=jnp.float32)
    grad_probs = jnp.einsum("ihd,jhd->hij", dout_heads, val_blk, preferred_element_type=jnp.float32)
    grad_scores = attn_probs * (grad_probs - row_delta[:, :, None])
    slope_add = -jnp.sum(grad_scores * lengths[None], axis=(1, 2))
    grad_b = grad_scores.astype(jnp.bfloat16)
    query_add = (
        jnp.einsum("hij,jhd->ihd", grad_b, key_blk, preferred_element_type=jnp.float32) * scale
    )
    key_add = (
        jnp.einsum("hij,ihd->jhd", grad_b, query_heads, preferred_element_type=jnp.float32) * scale
    )
    return (query_add, key_add, value_add, slope_add)


def per_device(query, key, value, attn_out, log_norm, d_output, out_weight, coords, slopes):
    row_count = query.shape[0]
    local_cols = query.shape[1]
    groups = local_cols // HEAD_DIM
    piece = lax.all_gather(d_output, "head", axis=1, tiled=True)
    grad_acc = lax.dot_general(
        piece, out_weight, (((1,), (1,)), ((), ())), preferred_element_type=jnp.float32
    )
    product = lax.dot_general(
        attn_out, piece, (((0,), (0,)), ((), ())), preferred_element_type=jnp.float32
    )
    weight_part = product
    grad_acc, weight_part = (grad_acc, weight_part)
    d_attn = grad_acc.astype(jnp.bfloat16)
    query_heads = query.reshape(row_count, groups, HEAD_DIM)
    key_heads = key.reshape(row_count, groups, HEAD_DIM)
    value_heads = value.reshape(row_count, groups, HEAD_DIM)
    dout_heads = d_attn.reshape(row_count, groups, HEAD_DIM)
    row_delta = jnp.sum(
        dout_heads.astype(jnp.float32)
        * attn_out.reshape(row_count, groups, HEAD_DIM).astype(jnp.float32),
        axis=2,
    ).T
    cycle_size = lax.axis_size("seq")
    zero_heads = jnp.zeros((row_count, groups, HEAD_DIM), jnp.float32)
    zero_rates = jnp.zeros((groups,), jnp.float32)

    def turn(carry):
        key_blk, val_blk, key_pos, key_grad, value_grad, query_grad, slope_grad = carry
        query_add, key_add, value_add, slope_add = attend(
            query_heads, dout_heads, row_delta, log_norm, slopes, key_blk, val_blk, coords, key_pos
        )
        return (
            key_blk,
            val_blk,
            key_pos,
            key_grad + key_add,
            value_grad + value_add,
            query_grad + query_add,
            slope_grad + slope_add,
        )

    def advance(index, carry):
        key_blk, val_blk, key_pos, key_grad, value_grad, query_grad, slope_grad = turn(carry)
        key_blk, val_blk, key_pos = from_behind((key_blk, val_blk, key_pos), "seq", 1)
        key_grad, value_grad = from_behind((key_grad, value_grad), "seq", 1)
        return (key_blk, val_blk, key_pos, key_grad, value_grad, query_grad, slope_grad)

    begin = (key_heads, value_heads, coords, zero_heads, zero_heads, zero_heads, zero_rates)
    final = turn(lax.fori_loop(0, cycle_size - 1, advance, begin))
    key_grad, value_grad = (
        from_behind(final[3].astype(jnp.bfloat16), "seq", 1).astype(jnp.float32),
        from_behind(final[4].astype(jnp.bfloat16), "seq", 1).astype(jnp.float32),
    )
    query_grad, slope_grad = (final[5], final[6])
    weight_sum, slope_sum = lax.psum((weight_part, slope_grad), "seq")
    d_query = query_grad.reshape(row_count, local_cols).astype(jnp.bfloat16)
    d_key = key_grad.reshape(row_count, local_cols).astype(jnp.bfloat16)
    d_value = value_grad.reshape(row_count, local_cols).astype(jnp.bfloat16)
    return (d_query, d_key, d_value, weight_sum, slope_sum)


def solution(mesh):
    placed = (
        P("seq", "head"),
        P("seq", "head"),
        P("seq", "head"),
        P("seq", "head"),
        P("head", "seq"),
        P("seq", "head"),
        P("head", None),
        P(None, "seq"),
        P("head"),
    )
    return jax.shard_map(
        per_device,
        mesh=mesh,
        in_specs=placed,
        out_specs=(
            P("seq", "head"),
            P("seq", "head"),
            P("seq", "head"),
            P("head", None),
            P("head"),
        ),
        check_vma=False,
    )
```

profile of v0, /device:TPU:0, one launch (start us, length us, event | category | flops | bytes accessed | tf_op | source)
XLA Modules:
  0.0 1305.2 jit_solution(13356308403050568075)
XLA Ops:
  7.3 9.0 all_gather.3
  21.3 908.4 %while.23 = (s32[]{:T(128)}, bf16[384,4,64]{0,2,1:T(8,128)(2,1)S(1)}, bf16[384,4,64]{0,2,1:T(8,128)(2,1)}, bf16[3,384]{1,0:T(4,128)(2,1)S(1)}, f32[384,4,64]{0,2...) while((s32[]{:T(128)}, ...), condition=%wide.region_3.0_spmd.clone, body=%wide.region_1.0_spmd.clone.sunk | while | flops 385304832 | bytes 21676468 | solution.py:99
  40.4 10.7 collective-permute-done.3
  51.1 6.9 collective-permute-done.4
  76.0 8.4 collective-permute-done.3
  84.4 6.0 collective-permute-done.4
  108.3 8.4 collective-permute-done.3
  139.6 8.4 collective-permute-done.3
  170.1 7.8 collective-permute-done.3
  200.1 7.0 collective-permute-done.3
  229.2 6.2 collective-permute-done.3
  285.6 6.7 collective-permute-done.3
  314.5 6.2 collective-permute-done.3
  342.8 7.3 collective-permute-done.3
  372.3 6.5 collective-permute-done.3
  428.7 8.0 collective-permute-done.3
  458.8 7.2 collective-permute-done.3
  488.3 6.4 collective-permute-done.3
  516.9 6.5 collective-permute-done.3
  573.4 6.9 collective-permute-done.3
  602.6 6.1 collective-permute-done.3
  659.0 8.3 collective-permute-done.3
  689.3 7.5 collective-permute-done.3
  719.1 6.7 collective-permute-done.3
  748.0 6.1 collective-permute-done.3
  776.3 6.0 collective-permute-done.3
  804.5 6.7 collective-permute-done.3
  861.4 7.2 collective-permute-done.3
  890.8 6.4 collective-permute-done.3
  919.4 6.0 collective-permute-done.3
  938.5 97.5 %psum.15 = f32[4]{0:T(128)} all-reduce(f32[4]{0:T(128)S(1)} %negate_add_fusion), channel_id=1, replica_groups=mesh['seq'=32,'head'=4] {'seq'}, use_global_device_ids=true, to_apply=%region_6.0 | all-reduce | flops 4 | bytes 32 | tf_op jit(solution)/shard_map/psum | solution.py:105
  1041.0 255.1 %all-reduce.2.cloned.1.call-done = f32[256,1024]{1,0:T(8,128)} async-done(((f32[256,1024]{1,0:T(8,128)}), f32[256,1024]{1,0:T(8,128)}) %all-reduce.2.cloned.1.call-update) | async-done | bytes 1048592 | tf_op jit(solution)/shard_map/psum | solution.py:105
  (678 shorter events, 729.8 us)
Async XLA Ops:
  7.2 1288.9 %all-reduce.2.cloned.1.call-start = ((), (), s32[]{:S(2)}) async-start(), calls=%async_computation | async-start | bytes 2097152 | tf_op jit(solution)/shard_map/psum | solution.py:105
  36.3 21.7 %collective-permute-start.4 = (f32[384,4,64]{0,2,1:T(8,128)}, f32[384,4,64]{0,2,1:T(8,128)S(1)}, u32[]{:S(2)}, u32[]{:S(2)}) collective-permute-start(f32[384,4,64]{0,2,1:T(8,128)} %fusion.72), channel_id=1, source_target_pairs={{124,0},{0,4},{4,8},{8,12},{12,16},{16,20},{20,24},{24,28},{28,32}... | collective-permute-start | bytes 1179656 | tf_op jit(solution)/shard_map/while/body/eval_jaxpr/ppermute | solution.py:12
  64.7 19.6 %collective-permute-start.3 = (f32[384,4,64]{0,2,1:T(8,128)}, f32[384,4,64]{0,2,1:T(8,128)S(1)}, u32[]{:S(2)}, u32[]{:S(2)}) collective-permute-start(f32[384,4,64]{0,2,1:T(8,128)} %fusion.71), channel_id=1, source_target_pairs={{124,0},{0,4},{4,8},{8,12},{12,16},{16,20},{20,24},{24,28},{28,32}... | collective-permute-start | bytes 1179656 | tf_op jit(solution)/shard_map/while/body/eval_jaxpr/ppermute | solution.py:12
  69.4 20.9 %collective-permute-start.4 = (f32[384,4,64]{0,2,1:T(8,128)}, f32[384,4,64]{0,2,1:T(8,128)S(1)}, u32[]{:S(2)}, u32[]{:S(2)}) collective-permute-start(f32[384,4,64]{0,2,1:T(8,128)} %fusion.72), channel_id=1, source_target_pairs={{124,0},{0,4},{4,8},{8,12},{12,16},{16,20},{20,24},{24,28},{28,32}... | collective-permute-start | bytes 1179656 | tf_op jit(solution)/shard_map/while/body/eval_jaxpr/ppermute | solution.py:12
  94.6 22.1 %collective-permute-start.3 = (f32[384,4,64]{0,2,1:T(8,128)}, f32[384,4,64]{0,2,1:T(8,128)S(1)}, u32[]{:S(2)}, u32[]{:S(2)}) collective-permute-start(f32[384,4,64]{0,2,1:T(8,128)} %fusion.71), channel_id=1, source_target_pairs={{124,0},{0,4},{4,8},{8,12},{12,16},{16,20},{20,24},{24,28},{28,32}... | collective-permute-start | bytes 1179656 | tf_op jit(solution)/shard_map/while/body/eval_jaxpr/ppermute | solution.py:12
  98.8 22.9 %collective-permute-start.4 = (f32[384,4,64]{0,2,1:T(8,128)}, f32[384,4,64]{0,2,1:T(8,128)S(1)}, u32[]{:S(2)}, u32[]{:S(2)}) collective-permute-start(f32[384,4,64]{0,2,1:T(8,128)} %fusion.72), channel_id=1, source_target_pairs={{124,0},{0,4},{4,8},{8,12},{12,16},{16,20},{20,24},{24,28},{28,32}... | collective-permute-start | bytes 1179656 | tf_op jit(solution)/shard_map/while/body/eval_jaxpr/ppermute | solution.py:12
  126.0 22.0 %collective-permute-start.3 = (f32[384,4,64]{0,2,1:T(8,128)}, f32[384,4,64]{0,2,1:T(8,128)S(1)}, u32[]{:S(2)}, u32[]{:S(2)}) collective-permute-start(f32[384,4,64]{0,2,1:T(8,128)} %fusion.71), channel_id=1, source_target_pairs={{124,0},{0,4},{4,8},{8,12},{12,16},{16,20},{20,24},{24,28},{28,32}... | collective-permute-start | bytes 1179656 | tf_op jit(solution)/shard_map/while/body/eval_jaxpr/ppermute | solution.py:12
  129.5 22.8 %collective-permute-start.4 = (f32[384,4,64]{0,2,1:T(8,128)}, f32[384,4,64]{0,2,1:T(8,128)S(1)}, u32[]{:S(2)}, u32[]{:S(2)}) collective-permute-start(f32[384,4,64]{0,2,1:T(8,128)} %fusion.72), channel_id=1, source_target_pairs={{124,0},{0,4},{4,8},{8,12},{12,16},{16,20},{20,24},{24,28},{28,32}... | collective-permute-start | bytes 1179656 | tf_op jit(solution)/shard_map/while/body/eval_jaxpr/ppermute | solution.py:12
  156.5 21.4 %collective-permute-start.3 = (f32[384,4,64]{0,2,1:T(8,128)}, f32[384,4,64]{0,2,1:T(8,128)S(1)}, u32[]{:S(2)}, u32[]{:S(2)}) collective-permute-start(f32[384,4,64]{0,2,1:T(8,128)} %fusion.71), channel_id=1, source_target_pairs={{124,0},{0,4},{4,8},{8,12},{12,16},{16,20},{20,24},{24,28},{28,32}... | collective-permute-start | bytes 1179656 | tf_op jit(solution)/shard_map/while/body/eval_jaxpr/ppermute | solution.py:12
  159.5 22.6 %collective-permute-start.4 = (f32[384,4,64]{0,2,1:T(8,128)}, f32[384,4,64]{0,2,1:T(8,128)S(1)}, u32[]{:S(2)}, u32[]{:S(2)}) collective-permute-start(f32[384,4,64]{0,2,1:T(8,128)} %fusion.72), channel_id=1, source_target_pairs={{124,0},{0,4},{4,8},{8,12},{12,16},{16,20},{20,24},{24,28},{28,32}... | collective-permute-start | bytes 1179656 | tf_op jit(solution)/shard_map/while/body/eval_jaxpr/ppermute | solution.py:12
  186.3 20.7 %collective-permute-start.3 = (f32[384,4,64]{0,2,1:T(8,128)}, f32[384,4,64]{0,2,1:T(8,128)S(1)}, u32[]{:S(2)}, u32[]{:S(2)}) collective-permute-start(f32[384,4,64]{0,2,1:T(8,128)} %fusion.71), channel_id=1, source_target_pairs={{124,0},{0,4},{4,8},{8,12},{12,16},{16,20},{20,24},{24,28},{28,32}... | collective-permute-start | bytes 1179656 | tf_op jit(solution)/shard_map/while/body/eval_jaxpr/ppermute | solution.py:12
  189.4 21.9 %collective-permute-start.4 = (f32[384,4,64]{0,2,1:T(8,128)}, f32[384,4,64]{0,2,1:T(8,128)S(1)}, u32[]{:S(2)}, u32[]{:S(2)}) collective-permute-start(f32[384,4,64]{0,2,1:T(8,128)} %fusion.72), channel_id=1, source_target_pairs={{124,0},{0,4},{4,8},{8,12},{12,16},{16,20},{20,24},{24,28},{28,32}... | collective-permute-start | bytes 1179656 | tf_op jit(solution)/shard_map/while/body/eval_jaxpr/ppermute | solution.py:12
  215.5 19.9 %collective-permute-start.3 = (f32[384,4,64]{0,2,1:T(8,128)}, f32[384,4,64]{0,2,1:T(8,128)S(1)}, u32[]{:S(2)}, u32[]{:S(2)}) collective-permute-start(f32[384,4,64]{0,2,1:T(8,128)} %fusion.71), channel_id=1, source_target_pairs={{124,0},{0,4},{4,8},{8,12},{12,16},{16,20},{20,24},{24,28},{28,32}... | collective-permute-start | bytes 1179656 | tf_op jit(solution)/shard_map/while/body/eval_jaxpr/ppermute | solution.py:12
  218.5 21.1 %collective-permute-start.4 = (f32[384,4,64]{0,2,1:T(8,128)}, f32[384,4,64]{0,2,1:T(8,128)S(1)}, u32[]{:S(2)}, u32[]{:S(2)}) collective-permute-start(f32[384,4,64]{0,2,1:T(8,128)} %fusion.72), channel_id=1, source_target_pairs={{124,0},{0,4},{4,8},{8,12},{12,16},{16,20},{20,24},{24,28},{28,32}... | collective-permute-start | bytes 1179656 | tf_op jit(solution)/shard_map/while/body/eval_jaxpr/ppermute | solution.py:12
  243.8 19.6 %collective-permute-start.3 = (f32[384,4,64]{0,2,1:T(8,128)}, f32[384,4,64]{0,2,1:T(8,128)S(1)}, u32[]{:S(2)}, u32[]{:S(2)}) collective-permute-start(f32[384,4,64]{0,2,1:T(8,128)} %fusion.71), channel_id=1, source_target_pairs={{124,0},{0,4},{4,8},{8,12},{12,16},{16,20},{20,24},{24,28},{28,32}... | collective-permute-start | bytes 1179656 | tf_op jit(solution)/shard_map/while/body/eval_jaxpr/ppermute | solution.py:12
  247.8 19.9 %collective-permute-start.4 = (f32[384,4,64]{0,2,1:T(8,128)}, f32[384,4,64]{0,2,1:T(8,128)S(1)}, u32[]{:S(2)}, u32[]{:S(2)}) collective-permute-start(f32[384,4,64]{0,2,1:T(8,128)} %fusion.72), channel_id=1, source_target_pairs={{124,0},{0,4},{4,8},{8,12},{12,16},{16,20},{20,24},{24,28},{28,32}... | collective-permute-start | bytes 1179656 | tf_op jit(solution)/shard_map/while/body/eval_jaxpr/ppermute | solution.py:12
  272.6 19.7 %collective-permute-start.3 = (f32[384,4,64]{0,2,1:T(8,128)}, f32[384,4,64]{0,2,1:T(8,128)S(1)}, u32[]{:S(2)}, u32[]{:S(2)}) collective-permute-start(f32[384,4,64]{0,2,1:T(8,128)} %fusion.71), channel_id=1, source_target_pairs={{124,0},{0,4},{4,8},{8,12},{12,16},{16,20},{20,24},{24,28},{28,32}... | collective-permute-start | bytes 1179656 | tf_op jit(solution)/shard_map/while/body/eval_jaxpr/ppermute | solution.py:12
  277.1 19.5 %collective-permute-start.4 = (f32[384,4,64]{0,2,1:T(8,128)}, f32[384,4,64]{0,2,1:T(8,128)S(1)}, u32[]{:S(2)}, u32[]{:S(2)}) collective-permute-start(f32[384,4,64]{0,2,1:T(8,128)} %fusion.72), channel_id=1, source_target_pairs={{124,0},{0,4},{4,8},{8,12},{12,16},{16,20},{20,24},{24,28},{28,32}... | collective-permute-start | bytes 1179656 | tf_op jit(solution)/shard_map/while/body/eval_jaxpr/ppermute | solution.py:12
  300.8 19.8 %collective-permute-start.3 = (f32[384,4,64]{0,2,1:T(8,128)}, f32[384,4,64]{0,2,1:T(8,128)S(1)}, u32[]{:S(2)}, u32[]{:S(2)}) collective-permute-start(f32[384,4,64]{0,2,1:T(8,128)} %fusion.71), channel_id=1, source_target_pairs={{124,0},{0,4},{4,8},{8,12},{12,16},{16,20},{20,24},{24,28},{28,32}... | collective-permute-start | bytes 1179656 | tf_op jit(solution)/shard_map/while/body/eval_jaxpr/ppermute | solution.py:12
  329.9 20.2 %collective-permute-start.3 = (f32[384,4,64]{0,2,1:T(8,128)}, f32[384,4,64]{0,2,1:T(8,128)S(1)}, u32[]{:S(2)}, u32[]{:S(2)}) collective-permute-start(f32[384,4,64]{0,2,1:T(8,128)} %fusion.71), channel_id=1, source_target_pairs={{124,0},{0,4},{4,8},{8,12},{12,16},{16,20},{20,24},{24,28},{28,32}... | collective-permute-start | bytes 1179656 | tf_op jit(solution)/shard_map/while/body/eval_jaxpr/ppermute | solution.py:12
  417.3 19.4 %collective-permute-start.3 = (f32[384,4,64]{0,2,1:T(8,128)}, f32[384,4,64]{0,2,1:T(8,128)S(1)}, u32[]{:S(2)}, u32[]{:S(2)}) collective-permute-start(f32[384,4,64]{0,2,1:T(8,128)} %fusion.71), channel_id=1, source_target_pairs={{124,0},{0,4},{4,8},{8,12},{12,16},{16,20},{20,24},{24,28},{28,32}... | collective-permute-start | bytes 1179656 | tf_op jit(solution)/shard_map/while/body/eval_jaxpr/ppermute | solution.py:12
  450.9 19.4 %collective-permute-start.4 = (f32[384,4,64]{0,2,1:T(8,128)}, f32[384,4,64]{0,2,1:T(8,128)S(1)}, u32[]{:S(2)}, u32[]{:S(2)}) collective-permute-start(f32[384,4,64]{0,2,1:T(8,128)} %fusion.72), channel_id=1, source_target_pairs={{124,0},{0,4},{4,8},{8,12},{12,16},{16,20},{20,24},{24,28},{28,32}... | collective-permute-start | bytes 1179656 | tf_op jit(solution)/shard_map/while/body/eval_jaxpr/ppermute | solution.py:12
  475.2 19.5 %collective-permute-start.3 = (f32[384,4,64]{0,2,1:T(8,128)}, f32[384,4,64]{0,2,1:T(8,128)S(1)}, u32[]{:S(2)}, u32[]{:S(2)}) collective-permute-start(f32[384,4,64]{0,2,1:T(8,128)} %fusion.71), channel_id=1, source_target_pairs={{124,0},{0,4},{4,8},{8,12},{12,16},{16,20},{20,24},{24,28},{28,32}... | collective-permute-start | bytes 1179656 | tf_op jit(solution)/shard_map/while/body/eval_jaxpr/ppermute | solution.py:12
  588.8 19.9 %collective-permute-start.3 = (f32[384,4,64]{0,2,1:T(8,128)}, f32[384,4,64]{0,2,1:T(8,128)S(1)}, u32[]{:S(2)}, u32[]{:S(2)}) collective-permute-start(f32[384,4,64]{0,2,1:T(8,128)} %fusion.71), channel_id=1, source_target_pairs={{124,0},{0,4},{4,8},{8,12},{12,16},{16,20},{20,24},{24,28},{28,32}... | collective-permute-start | bytes 1179656 | tf_op jit(solution)/shard_map/while/body/eval_jaxpr/ppermute | solution.py:12
  677.4 19.5 %collective-permute-start.3 = (f32[384,4,64]{0,2,1:T(8,128)}, f32[384,4,64]{0,2,1:T(8,128)S(1)}, u32[]{:S(2)}, u32[]{:S(2)}) collective-permute-start(f32[384,4,64]{0,2,1:T(8,128)} %fusion.71), channel_id=1, source_target_pairs={{124,0},{0,4},{4,8},{8,12},{12,16},{16,20},{20,24},{24,28},{28,32}... | collective-permute-start | bytes 1179656 | tf_op jit(solution)/shard_map/while/body/eval_jaxpr/ppermute | solution.py:12
  681.5 19.6 %collective-permute-start.4 = (f32[384,4,64]{0,2,1:T(8,128)}, f32[384,4,64]{0,2,1:T(8,128)S(1)}, u32[]{:S(2)}, u32[]{:S(2)}) collective-permute-start(f32[384,4,64]{0,2,1:T(8,128)} %fusion.72), channel_id=1, source_target_pairs={{124,0},{0,4},{4,8},{8,12},{12,16},{16,20},{20,24},{24,28},{28,32}... | collective-permute-start | bytes 1179656 | tf_op jit(solution)/shard_map/while/body/eval_jaxpr/ppermute | solution.py:12
  710.5 19.5 %collective-permute-start.4 = (f32[384,4,64]{0,2,1:T(8,128)}, f32[384,4,64]{0,2,1:T(8,128)S(1)}, u32[]{:S(2)}, u32[]{:S(2)}) collective-permute-start(f32[384,4,64]{0,2,1:T(8,128)} %fusion.72), channel_id=1, source_target_pairs={{124,0},{0,4},{4,8},{8,12},{12,16},{16,20},{20,24},{24,28},{28,32}... | collective-permute-start | bytes 1179656 | tf_op jit(solution)/shard_map/while/body/eval_jaxpr/ppermute | solution.py:12
  738.7 19.6 %collective-permute-start.4 = (f32[384,4,64]{0,2,1:T(8,128)}, f32[384,4,64]{0,2,1:T(8,128)S(1)}, u32[]{:S(2)}, u32[]{:S(2)}) collective-permute-start(f32[384,4,64]{0,2,1:T(8,128)} %fusion.72), channel_id=1, source_target_pairs={{124,0},{0,4},{4,8},{8,12},{12,16},{16,20},{20,24},{24,28},{28,32}... | collective-permute-start | bytes 1179656 | tf_op jit(solution)/shard_map/while/body/eval_jaxpr/ppermute | solution.py:12
  762.6 19.8 %collective-permute-start.3 = (f32[384,4,64]{0,2,1:T(8,128)}, f32[384,4,64]{0,2,1:T(8,128)S(1)}, u32[]{:S(2)}, u32[]{:S(2)}) collective-permute-start(f32[384,4,64]{0,2,1:T(8,128)} %fusion.71), channel_id=1, source_target_pairs={{124,0},{0,4},{4,8},{8,12},{12,16},{16,20},{20,24},{24,28},{28,32}... | collective-permute-start | bytes 1179656 | tf_op jit(solution)/shard_map/while/body/eval_jaxpr/ppermute | solution.py:12
  877.1 20.2 %collective-permute-start.3 = (f32[384,4,64]{0,2,1:T(8,128)}, f32[384,4,64]{0,2,1:T(8,128)S(1)}, u32[]{:S(2)}, u32[]{:S(2)}) collective-permute-start(f32[384,4,64]{0,2,1:T(8,128)} %fusion.71), channel_id=1, source_target_pairs={{124,0},{0,4},{4,8},{8,12},{12,16},{16,20},{20,24},{24,28},{28,32}... | collective-permute-start | bytes 1179656 | tf_op jit(solution)/shard_map/while/body/eval_jaxpr/ppermute | solution.py:12
  934.0 104.4 %collective-permute-start.6 = (bf16[384,4,64]{0,2,1:T(8,128)(2,1)}, bf16[384,4,64]{0,2,1:T(8,128)(2,1)}, u32[]{:S(2)}, u32[]{:S(2)}) collective-permute-start(bf16[384,4,64]{0,2,1:T(8,128)(2,1)} %fusion.19), channel_id=1, source_target_pairs={{124,0},{0,4},{4,8},{8,12},{12,16},{16,20},{20,24},{24,28},{28,32}... | collective-permute-start | bytes 589832 | tf_op jit(solution)/shard_map/ppermute | solution.py:12
  938.5 101.7 %collective-permute-start.5 = (bf16[384,4,64]{0,2,1:T(8,128)(2,1)S(1)}, bf16[384,4,64]{0,2,1:T(8,128)(2,1)S(1)}, u32[]{:S(2)}, u32[]{:S(2)}) collective-permute-start(bf16[384,4,64]{0,2,1:T(8,128)(2,1)S(1)} %fusion.17), channel_id=1, source_target_pairs={{124,0},{0,4},{4,8},{8,12},{12,16},{16,20},{20,24},{24,28},{28,32}... | collective-permute-start | bytes 589832 | tf_op jit(solution)/shard_map/ppermute | solution.py:12
  (139 other events, 2271.6 us)
Sparse Core Ops, SparseCore 0:
  935.6 360.4 all-reduce.1
where the time goes:
time: 1310 us
  waiting for transfers between devices  679 us (52%)
  starting transfers between devices  253 us (19%)
  matrix products  197 us (15%)
  blocking collectives  107 us (8%)
  local copies, waits for them, and re-layouts  40.2 us (3%)
  other arithmetic  14.5 us (1%)
  between operations  14.2 us (1%)
    ppermute x157, waiting for transfers between devices, from_behind(): return lax.ppermute(block, axis, route)  424 us
    psum x1, waiting for transfers between devices, per_device(): weight_sum, slope_sum = lax.psum((weight_part, slope_grad), 'seq')  255 us
    ppermute x157, starting transfers between devices, from_behind(): return lax.ppermute(block, axis, route)  253 us
    psum x1, blocking collectives, per_device(): weight_sum, slope_sum = lax.psum((weight_part, slope_grad), 'seq')  97.5 us
    dot_general x32, matrix products, attend(): jnp.einsum('hij,jhd->ihd', grad_b, key_blk, preferred_element_type=jnp.fl...  71.4 us
    dot_general x32, matrix products, attend(): jnp.einsum('hij,ihd->jhd', probs_b, dout_heads, preferred_element_type=jn...  34.7 us
    dot_general x32, matrix products, attend(): jnp.einsum('hij,ihd->jhd', grad_b, query_heads, preferred_element_type=jn...  33.5 us
    dot_general x32, matrix products, attend(): jnp.einsum('ihd,jhd->hij', dout_heads, val_blk, preferred_element_type=jn...  30.1 us
  transfers between devices with their start and end apart: 158, of which 93 were waited for; matrix products, arithmetic and copies ran while one was open for 18% of the time, Pallas kernels for 0%

commit v1 on v0

v1 whole, which is shorter than its diff:
```python
import functools

import jax
import jax.numpy as jnp
from jax import lax
from jax.experimental import pallas as pl
from jax.experimental.pallas import tpu as pltpu
from jax.sharding import PartitionSpec as P

HEAD_DIM = 64
LOG2E = 1.4426950408889634
f32 = jnp.float32
bf16 = jnp.bfloat16
AXES = ("seq", "head")


def dot(a, b, dims=((1,), (0,))):
    return lax.dot_general(a, b, (dims, ((), ())), preferred_element_type=f32)


def split3(x):
    a = x.astype(bf16).astype(f32)
    r = x - a
    b = r.astype(bf16).astype(f32)
    return a, b, r - b


def prep_query(q, do, sm, aug, qa, doa, q_t, do_t):
    n = q.shape[0]
    rows = []
    for h in range(2):
        rows += list(split3(sm[h : h + 1, :] * (-8.0)))
    for h in range(2):
        rows += list(split3(-sm[2 + h : 3 + h, :]))
    c = [sm[4 + d : 5 + d, :] for d in range(3)]
    rows += c
    rows += list(split3(1.0 + (c[0] * c[0] + c[1] * c[1] + c[2] * c[2])))
    rows += [jnp.ones((1, n), f32)] * 3
    rows += [jnp.zeros((24 - len(rows), n), f32)]
    top = jnp.concatenate(rows, axis=0)
    fill = jnp.zeros((40, n), f32)
    a = jnp.concatenate([top, fill, top, fill], axis=0).T.astype(bf16)
    aug[...] = a
    low = lax.broadcasted_iota(jnp.int32, (n, 128), 1) < HEAD_DIM
    qa[0] = jnp.where(low, q, a)
    qa[1] = jnp.where(low, a, q)
    doa[0] = jnp.where(low, do, a)
    doa[1] = jnp.where(low, a, do)
    q_t[...] = q.T
    do_t[...] = do.T


def prep_key(k, v, cj, ka_t, va_t, ca_t, k_t):
    n = k.shape[0]
    kt = k.T
    vt = v.T
    k_t[...] = kt
    row = lax.broadcasted_iota(jnp.int32, (128, n), 0)
    low = row < HEAD_DIM
    pos = jnp.where(low, row, row - HEAD_DIM)

    def pick(start):
        hit = (pos >= start) & (pos < start + 3)
        return jnp.where(hit, 1.0, 0.0).astype(bf16)

    ka_t[0] = jnp.where(low, kt, pick(0))
    ka_t[1] = jnp.where(low, pick(3), kt)
    va_t[0] = jnp.where(low, vt, pick(6))
    va_t[1] = jnp.where(low, pick(9), vt)
    c = [cj[d : d + 1, :] for d in range(3)]
    m = split3(c[0] * c[0] + c[1] * c[1] + c[2] * c[2])
    ca = jnp.concatenate(
        [jnp.zeros((12, n), f32)]
        + [-2.0 * x for x in c]
        + [jnp.ones((3, n), f32)]
        + list(m)
        + [jnp.zeros((128 - 21, n), f32)],
        axis=0,
    )
    ca_t[...] = ca.astype(bf16)


def tile(qa, doa, aug, q_t, do_t, ka_t, va_t, ca_t, k_t, rates, dq_t, dk_t, dv_t, ds, i, j, bi, bj):
    ii = pl.ds(i, bi)
    jj = pl.ds(j, bj)
    l2 = jnp.maximum(dot(aug[ii, :], ca_t[:, jj]), 1.0)
    lengths = l2 * lax.rsqrt(l2)
    ps = []
    gs = []
    for h in range(2):
        s = dot(qa[h, ii, :], ka_t[h, :, jj])
        gp = dot(doa[h, ii, :], va_t[h, :, jj])
        p = jnp.exp2(s * (LOG2E / 8.0) - lengths * rates[h])
        g = p * gp
        ds[h] += jnp.sum((g * lengths).reshape(bi // 8, 8, bj), axis=0)
        ps.append(p.astype(bf16))
        gs.append(g.astype(bf16))
    for h in range(2):
        hh = pl.ds(h * HEAD_DIM, HEAD_DIM)
        dv_t[hh, jj] += dot(do_t[hh, ii], ps[h])
        dk_t[hh, jj] += dot(q_t[hh, ii], gs[h])
        dq_t[hh, ii] += dot(k_t[hh, jj], gs[h], ((1,), (1,)))


def attend_kernel(
    bi, bj, q, do, sm, k, v, cj,
    dq_out, dk_out, dv_out, ds_out,
    aug, qa, doa, q_t, do_t, ka_t, va_t, ca_t, k_t, dq_t, dk_t, dv_t, ds,
):
    ns, n, _ = q.shape
    dq_t[...] = jnp.zeros_like(dq_t)
    dk_t[...] = jnp.zeros_like(dk_t)
    dv_t[...] = jnp.zeros_like(dv_t)
    ds[...] = jnp.zeros_like(ds)

    def prep(s, _):
        prep_query(
            q[s], do[s], sm[s], aug.at[s], qa.at[s], doa.at[s], q_t.at[s], do_t.at[s]
        )
        prep_key(k[s], v[s], cj[s], ka_t.at[s], va_t.at[s], ca_t.at[s], k_t.at[s])
        return 0

    lax.fori_loop(0, ns, prep, 0)
    rates = [
        jnp.concatenate([sm[0, 7:8, h * 128 : (h + 1) * 128]] * (bj // 128), axis=1) * LOG2E
        for h in range(2)
    ]

    def body(t, _):
        si = t // ns
        sj = t % ns
        nj = n // bj

        def step(u, _):
            i = pl.multiple_of((u // nj) * bi, bi)
            j = pl.multiple_of((u % nj) * bj, bj)
            tile(
                qa.at[si], doa.at[si], aug.at[si], q_t.at[si], do_t.at[si],
                ka_t.at[sj], va_t.at[sj], ca_t.at[sj], k_t.at[sj], rates,
                dq_t.at[si], dk_t.at[sj], dv_t.at[sj], ds, i, j, bi, bj,
            )
            return 0

        lax.fori_loop(0, (n // bi) * nj, step, 0)
        return 0

    lax.fori_loop(0, ns * ns, body, 0)
    dq_out[...] = (dq_t[...] * 0.125).astype(bf16)
    dk_out[...] = (dk_t[...] * 0.125).astype(bf16)
    dv_out[...] = dv_t[...].astype(bf16)
    for h in range(2):
        total = jnp.sum(ds[h], axis=0, keepdims=True)
        total = jnp.sum(total, axis=1, keepdims=True)
        ds_out[h : h + 1, :] = jnp.broadcast_to(-total, (1, 128))


def attend(q, do, sm, k, v, cj, bi, bj):
    ns, n, _ = q.shape
    vm = pl.BlockSpec(memory_space=pltpu.VMEM)

    def wide(*lead):
        return pltpu.VMEM(lead + (n, 128), bf16)

    def tall(dtype, *lead):
        return pltpu.VMEM(lead + (128, n), dtype)

    return pl.pallas_call(
        functools.partial(attend_kernel, bi, bj),
        out_shape=[jax.ShapeDtypeStruct((ns, 128, n), bf16)] * 3
        + [jax.ShapeDtypeStruct((2, 128), f32)],
        in_specs=[vm] * 6,
        out_specs=[vm] * 4,
        scratch_shapes=[
            wide(ns), wide(ns, 2), wide(ns, 2), tall(bf16, ns), tall(bf16, ns),
            tall(bf16, ns, 2), tall(bf16, ns, 2), tall(bf16, ns), tall(bf16, ns),
            tall(f32, ns), tall(f32, ns), tall(f32, ns), pltpu.VMEM((2, 8, bj), f32),
        ],
        compiler_params=pltpu.CompilerParams(vmem_limit_bytes=60 << 20),
        name="attend",
    )(q, do, sm, k, v, cj)


def devices():
    for y in range(4):
        for z in range(4):
            for xh in range(2):
                for xl in range(2):
                    for c in range(2):
                        yield y, z, xh, xl, c


def number(y, z, xh, xl, c):
    return ((y % 4 * 4 + z % 4) * 2 + xh) * 4 + xl * 2 + c


def permute(x, move):
    return lax.ppermute(x, AXES, [(number(*d), number(*move(*d))) for d in devices()])


def cross_a(x):
    return permute(x, lambda y, z, xh, xl, c: (y, z, xh, 1 - xl, c))


def cross_b(x):
    return permute(x, lambda y, z, xh, xl, c: (y, z, 1 - xh, 1 - xl, c))


def along_z(x, s):
    return permute(x, lambda y, z, xh, xl, c: (y, z + s, xh, xl, c))


def along_y(x, s):
    return permute(x, lambda y, z, xh, xl, c: (y + s, z, xh, xl, c))


def exchange(x, xh, axis):
    near = cross_a(lax.dynamic_index_in_dim(x, xh, 0, False))
    far = cross_b(lax.dynamic_index_in_dim(x, 1 - xh, 0, False))
    return jnp.concatenate([near, far], axis=axis)


def give_back(x, xh, rows):
    near = cross_a(x[:, :rows])
    far = cross_b(x[:, rows:])
    first = jnp.where(xh == 0, near, far)
    second = jnp.where(xh == 0, far, near)
    return jnp.concatenate([first, second], axis=0).T


def spread(x, shift):
    return jnp.stack([x] + [shift(x, s) for s in (1, 2, 3)])


def collect(parts, shift):
    total = parts[0].astype(f32)
    for s in (1, 2, 3):
        total = total + shift(parts[s], -s).astype(f32)
    return total.astype(bf16)


def per_device(query, key, value, attn_out, log_norm, d_output, out_weight, coords, slopes):
    rows, cols = query.shape
    groups = cols // HEAD_DIM
    seq = lax.axis_index("seq")
    head = lax.axis_index("head")
    xh = seq % 2

    def pairs(x):
        return x.reshape(rows, 2, 128).transpose(1, 0, 2)

    k = spread(exchange(pairs(key), xh, 0), along_y)
    v = spread(exchange(pairs(value), xh, 0), along_y)
    q = spread(exchange(pairs(query), xh, 0), along_z)

    piece = lax.all_gather(d_output, "head", axis=1, tiled=True)
    d_attn = dot(piece, out_weight, ((1,), (1,))).astype(bf16)
    delta = jnp.sum(
        (d_attn.astype(f32) * attn_out.astype(f32)).reshape(rows, groups, HEAD_DIM), axis=2
    ).T
    do = spread(exchange(pairs(d_attn), xh, 0), along_z)
    pos = coords.astype(f32)
    rates = slopes.reshape(2, 2)
    rate_row = jnp.concatenate(
        [jnp.broadcast_to(rates[:, h : h + 1], (2, 128)) for h in range(2)]
        + [jnp.zeros((2, rows - 256), f32)],
        axis=1,
    )
    small = jnp.concatenate(
        [
            log_norm.reshape(2, 2, rows),
            delta.reshape(2, 2, rows),
            jnp.broadcast_to(pos[None], (2, 3, rows)),
            rate_row[:, None],
        ],
        axis=1,
    )
    small = exchange(small, xh, 1)
    sm = spread(small, along_z)
    cj = spread(small[4:], along_y)
    dq, dk, dv, ds = attend(q, do, sm, k, v, jnp.concatenate([cj, cj], axis=1), 768, 768)
    d_query = give_back(collect(dq, along_z), xh, rows)
    d_key = give_back(collect(dk, along_y), xh, rows)
    d_value = give_back(collect(dv, along_y), xh, rows)

    weight_part = dot(attn_out, piece, ((0,), (0,)))
    weight_sum = lax.psum(weight_part, "seq")
    first = (head ^ 2) * 4 + xh * 2
    place = jnp.arange(16)
    mine = jnp.where(place == first, ds[0, 0], 0.0) + jnp.where(place == first + 1, ds[1, 0], 0.0)
    slope_sum = lax.psum(mine, AXES)
    slope_sum = lax.dynamic_slice_in_dim(slope_sum, head * groups, groups)
    return (d_query, d_key, d_value, weight_sum, slope_sum)


def solution(mesh):
    placed = (
        P("seq", "head"),
        P("seq", "head"),
        P("seq", "head"),
        P("seq", "head"),
        P("head", "seq"),
        P("seq", "head"),
        P("head", None),
        P(None, "seq"),
        P("head"),
    )
    return jax.shard_map(
        per_device,
        mesh=mesh,
        in_specs=placed,
        out_specs=(
            P("seq", "head"),
            P("seq", "head"),
            P("seq", "head"),
            P("head", None),
            P("head"),
        ),
        check_vma=False,
    )
```

time: 1310 us -> 393 us (0.30)
  waiting for transfers between devices: 679 us -> 155 us
  matrix products: 197 us -> 1.9 us
  starting transfers between devices: 253 us -> 62.2 us
  Pallas kernels: 0 us -> 66.1 us
  blocking collectives: 107 us -> 72.2 us
  local copies, waits for them, and re-layouts: 40.2 us -> 13.3 us
    ppermute x157 -> x43, waiting for transfers between devices: 424 us -> 24.5 us  [permute(): lax.ppermute(x, AXES, [(number(*d), number(*move(*d))) for d in devices()])]
    dot_general x162 -> x2, matrix products: 197 us -> 1.9 us  [dot(): return lax.dot_general(a, b, (dims, ((), ())), preferred_element_type=f32)]
    ppermute x157 -> x43, starting transfers between devices: 253 us -> 62.1 us  [permute(): lax.ppermute(x, AXES, [(number(*d), number(*move(*d))) for d in devices()])]
    psum x1, waiting for transfers between devices: 255 us -> 130 us  [per_device(): weight_sum = lax.psum(weight_part, 'seq')]
    pallas_call x0 -> x1, Pallas kernels: none -> 66.1 us  [attend(): pl.pallas_call(functools.partial(attend_kernel, bi, bj), out_shape=[jax.S...]
    psum x1, blocking collectives: 97.5 us -> 63.2 us  [per_device(): slope_sum = lax.psum(mine, AXES)]
    while x93 -> x0, local copies, waits for them, and re-layouts: 29.6 us -> none
  transfers between devices with their start and end apart: 158 -> 44, of which waited for: 93 -> 13; matrix products, arithmetic and copies ran while one was open for 18% -> 4% of each run, Pallas kernels for 0% -> 17%
where the time goes in v1:
time: 393 us
  waiting for transfers between devices  155 us (39%)
  blocking collectives  72.2 us (18%)
  Pallas kernels  66.1 us (17%)
  starting transfers between devices  62.2 us (16%)
  between operations  14.5 us (4%)
  local copies, waits for them, and re-layouts  13.3 us (3%)
  other arithmetic  7.98 us (2%)
    psum x1, waiting for transfers between devices, per_device(): weight_sum = lax.psum(weight_part, 'seq')  130 us
    pallas_call x1, Pallas kernels, attend(): pl.pallas_call(functools.partial(attend_kernel, bi, bj), out_shape=[jax.S...  66.1 us
    psum x1, blocking collectives, per_device(): slope_sum = lax.psum(mine, AXES)  63.2 us
    ppermute x43, starting transfers between devices, permute(): lax.ppermute(x, AXES, [(number(*d), number(*move(*d))) for d in devices()])  62.1 us
    ppermute x43, waiting for transfers between devices, permute(): lax.ppermute(x, AXES, [(number(*d), number(*move(*d))) for d in devices()])  24.5 us
    all_gather x1, blocking collectives, per_device(): piece = lax.all_gather(d_output, 'head', axis=1, tiled=True)  9.02 us
    unnamed x38, local copies, waits for them, and re-layouts  8.23 us
  transfers between devices with their start and end apart: 44, of which 13 were waited for; matrix products, arithmetic and copies ran while one was open for 4% of the time, Pallas kernels for 17%

profile of v1, /device:TPU:0, one launch (start us, length us, event | category | flops | bytes accessed | tf_op | source)
XLA Modules:
  0.0 392.9 jit_solution(9389377321811791423)
XLA Ops:
  7.3 9.0 %all_gather.3 = bf16[384,1024]{1,0:T(8,128)(2,1)S(1)} all-gather(bf16[384,256]{1,0:T(8,128)(2,1)} %param.14), channel_id=1, replica_groups=mesh['seq'=32,'head'=4] {'head'}, dimensions={1}, use_global_device_ids=true | all-gather | bytes 983040 | tf_op jit(solution)/shard_map/all_gather | solution.py:255
  20.7 2.2 collective-permute-start.11
  24.4 1.5 collective-permute-start.21
  28.8 1.6 collective-permute-start.25
  30.5 2.9 collective-permute-start.26
  35.1 2.0 collective-permute-start.12
  37.1 3.6 collective-permute-start.13
  42.9 2.2 collective-permute-start.16
  46.2 1.7 collective-permute-start.6
  48.5 2.1 collective-permute-start.1
  52.9 1.7 collective-permute-start.23
  56.9 1.9 collective-permute-start.18
  58.7 5.1 %collective-permute-done.22 = bf16[768,128]{1,0:T(8,128)(2,1)S(1)} collective-permute-done((bf16[768,128]{1,0:T(8,128)(2,1)S(1)}, bf16[768,128]{1,0:T(8,128)(2,1)S(1)}, u32[]{:S(2)}, u32[]{:S(2)}) %collective-permute-start.22) | collective-permute-done | bytes 196640 | tf_op jit(solution)/shard_map/ppermute | solution.py:197
  65.0 3.1 collective-permute-start.8
  68.1 3.2 collective-permute-start.9
  73.8 1.8 collective-permute-start.4
  76.7 1.8 collective-permute-done.8
  80.8 2.5 collective-permute-done.2
  84.3 66.1 %attend.1 = (bf16[4,128,768]{2,1,0:T(8,128)(2,1)}, bf16[4,128,768]{2,1,0:T(8,128)(2,1)}, bf16[4,128,768]{2,1,0:T(8,128)(2,1)}, f32[2,128]{1,0:T(2,128)}) custom-call(bf16[4,768,128]{2,1,0:T(8,128)(2,1)} %pad_maximum_fusion.q, bf16[4,768,128]{2,1,0:T(8,128)(2,1)} %pad_maximum_fusion.1.do, f32[4,8,768]{2,1,0:T(8,128)} %pad_maximum_fusion.4.sm, ...), custom_call_target="tpu_custom_call" | custom-call | tf_op jit(solution)/shard_map/attend/pallas_call | solution.py:167
  153.0 63.2 %psum.15 = f32[16]{0:T(128)S(1)} all-reduce(f32[16]{0:T(128)S(1)} %fusion.9), channel_id=1, replica_groups=mesh['seq'=32,'head'=4] {'seq','head'}, use_global_device_ids=true, to_apply=%region_2.3 | all-reduce | flops 16 | bytes 128 | tf_op jit(solution)/shard_map/psum | solution.py:290
  217.3 2.1 collective-permute-start.38
  220.9 2.8 collective-permute-start.33
  225.7 3.1 collective-permute-done.38
  228.8 2.0 collective-permute-start.28
  230.8 2.2 collective-permute-done.40
  233.0 2.4 collective-permute-start.29
  236.4 1.7 collective-permute-start.30
  239.9 1.6 collective-permute-start.42
  243.9 1.8 collective-permute-done.30
  250.7 1.9 collective-permute-done.32
  253.5 130.3 %all-reduce.2.cloned.1.call-done = f32[256,1024]{1,0:T(8,128)} async-done(((f32[256,1024]{1,0:T(8,128)}), f32[256,1024]{1,0:T(8,128)}) %all-reduce.2.cloned.1.call-update) | async-done | bytes 1048592 | tf_op jit(solution)/shard_map/psum | solution.py:286
  383.8 2.3 copy.64
  (149 shorter events, 45.0 us)
Async XLA Ops:
  7.2 376.6 %all-reduce.2.cloned.1.call-start = ((), (), s32[]{:S(2)}) async-start(), calls=%async_computation | async-start | bytes 2097152 | tf_op jit(solution)/shard_map/psum | solution.py:286
  19.5 9.3 %collective-permute-start.10 = (f32[8,384]{1,0:T(8,128)S(1)}, f32[8,384]{1,0:T(8,128)S(1)}, u32[]{:S(2)}, u32[]{:S(2)}) collective-permute-start(f32[8,384]{1,0:T(8,128)S(1)} %get-tuple-element.57), channel_id=1, source_target_pairs={{0,2},{1,3},{2,0},{3,1},{4,6},{5,7},{6,4},{7,5},{8,10},{9,11},{10,... | collective-permute-start | bytes 36872 | tf_op jit(solution)/shard_map/ppermute | solution.py:197
  20.7 8.2 %collective-permute-start.11 = (f32[8,384]{1,0:T(8,128)S(1)}, f32[8,384]{1,0:T(8,128)S(1)}, u32[]{:S(2)}, u32[]{:S(2)}) collective-permute-start(f32[8,384]{1,0:T(8,128)S(1)} %get-tuple-element.56), channel_id=1, source_target_pairs={{0,6},{1,7},{2,4},{3,5},{4,2},{5,3},{6,0},{7,1},{8,14},{9,15},{10,... | collective-permute-start | bytes 36872 | tf_op jit(solution)/shard_map/ppermute | solution.py:197
  23.8 22.4 %collective-permute-start.20 = (bf16[384,128]{1,0:T(8,128)(2,1)S(1)}, bf16[384,128]{1,0:T(8,128)(2,1)S(1)}, u32[]{:S(2)}, u32[]{:S(2)}) collective-permute-start(bf16[384,128]{1,0:T(8,128)(2,1)S(1)} %bitcast.113), channel_id=1, source_target_pairs={{0,2},{1,3},{2,0},{3,1},{4,6},{5,7},{6,4},{7,5},{8,10},{9,11},{10,... | collective-permute-start | bytes 294920 | tf_op jit(solution)/shard_map/ppermute | solution.py:197
  24.4 24.1 %collective-permute-start.21 = (bf16[384,128]{1,0:T(8,128)(2,1)S(1)}, bf16[384,128]{1,0:T(8,128)(2,1)S(1)}, u32[]{:S(2)}, u32[]{:S(2)}) collective-permute-start(bf16[384,128]{1,0:T(8,128)(2,1)S(1)} %bitcast.112), channel_id=1, source_target_pairs={{0,6},{1,7},{2,4},{3,5},{4,2},{5,3},{6,0},{7,1},{8,14},{9,15},{10,... | collective-permute-start | bytes 294920 | tf_op jit(solution)/shard_map/ppermute | solution.py:197
  33.4 7.3 %collective-permute-start.27 = (f32[4,768]{1,0:T(4,128)S(1)}, f32[4,768]{1,0:T(4,128)S(1)}, u32[]{:S(2)}, u32[]{:S(2)}) collective-permute-start(f32[4,768]{1,0:T(4,128)S(1)} %get-tuple-element.55), channel_id=1, source_target_pairs={{0,96},{1,97},{2,98},{3,99},{4,100},{5,101},{6,102},{7,103},{8,104... | collective-permute-start | bytes 36872 | tf_op jit(solution)/shard_map/ppermute | solution.py:197
  42.9 11.7 %collective-permute-start.16 = (bf16[384,128]{1,0:T(8,128)(2,1)S(1)}, bf16[384,128]{1,0:T(8,128)(2,1)S(1)}, u32[]{:S(2)}, u32[]{:S(2)}) collective-permute-start(bf16[384,128]{1,0:T(8,128)(2,1)S(1)} %bitcast.115), channel_id=1, source_target_pairs={{0,6},{1,7},{2,4},{3,5},{4,2},{5,3},{6,0},{7,1},{8,14},{9,15},{10,... | collective-permute-start | bytes 294920 | tf_op jit(solution)/shard_map/ppermute | solution.py:197
  46.2 9.9 %collective-permute-start.6 = (bf16[384,128]{1,0:T(8,128)(2,1)S(1)}, bf16[384,128]{1,0:T(8,128)(2,1)S(1)}, u32[]{:S(2)}, u32[]{:S(2)}) collective-permute-start(bf16[384,128]{1,0:T(8,128)(2,1)S(1)} %bitcast.109), channel_id=1, source_target_pairs={{0,6},{1,7},{2,4},{3,5},{4,2},{5,3},{6,0},{7,1},{8,14},{9,15},{10,... | collective-permute-start | bytes 294920 | tf_op jit(solution)/shard_map/ppermute | solution.py:197
  48.5 8.3 %collective-permute-start.1 = (bf16[384,128]{1,0:T(8,128)(2,1)S(1)}, bf16[384,128]{1,0:T(8,128)(2,1)S(1)}, u32[]{:S(2)}, u32[]{:S(2)}) collective-permute-start(bf16[384,128]{1,0:T(8,128)(2,1)S(1)} %bitcast.114), channel_id=1, source_target_pairs={{0,6},{1,7},{2,4},{3,5},{4,2},{5,3},{6,0},{7,1},{8,14},{9,15},{10,... | collective-permute-start | bytes 294920 | tf_op jit(solution)/shard_map/ppermute | solution.py:197
  50.6 13.2 %collective-permute-start.22 = (bf16[768,128]{1,0:T(8,128)(2,1)S(1)}, bf16[768,128]{1,0:T(8,128)(2,1)S(1)}, u32[]{:S(2)}, u32[]{:S(2)}) collective-permute-start(bf16[768,128]{1,0:T(8,128)(2,1)S(1)} %constant_dynamic-update-slice_fusion.8), channel_id=1, source_target_pairs={{0,32},{1,33},{2,34},{3,35},{4,36},{5,37},{6,38},{7,39},{8,40},{9,... | collective-permute-start | bytes 589832 | tf_op jit(solution)/shard_map/ppermute | solution.py:197
  52.9 10.9 %collective-permute-start.23 = (bf16[768,128]{1,0:T(8,128)(2,1)S(1)}, bf16[768,128]{1,0:T(8,128)(2,1)S(1)}, u32[]{:S(2)}, u32[]{:S(2)}) collective-permute-start(bf16[768,128]{1,0:T(8,128)(2,1)S(1)} %constant_dynamic-update-slice_fusion.8), channel_id=1, source_target_pairs={{0,64},{1,65},{2,66},{3,67},{4,68},{5,69},{6,70},{7,71},{8,72},{9,... | collective-permute-start | bytes 589832 | tf_op jit(solution)/shard_map/ppermute | solution.py:197
  54.6 10.4 %collective-permute-start.24 = (bf16[768,128]{1,0:T(8,128)(2,1)S(1)}, bf16[768,128]{1,0:T(8,128)(2,1)S(1)}, u32[]{:S(2)}, u32[]{:S(2)}) collective-permute-start(bf16[768,128]{1,0:T(8,128)(2,1)S(1)} %constant_dynamic-update-slice_fusion.8), channel_id=1, source_target_pairs={{0,96},{1,97},{2,98},{3,99},{4,100},{5,101},{6,102},{7,103},{8,104... | collective-permute-start | bytes 589832 | tf_op jit(solution)/shard_map/ppermute | solution.py:197
  56.2 12.0 %collective-permute-start.17 = (bf16[768,128]{1,0:T(8,128)(2,1)S(1)}, bf16[768,128]{1,0:T(8,128)(2,1)S(1)}, u32[]{:S(2)}, u32[]{:S(2)}) collective-permute-start(bf16[768,128]{1,0:T(8,128)(2,1)S(1)} %constant_dynamic-update-slice_fusion.6), channel_id=1, source_target_pairs={{0,32},{1,33},{2,34},{3,35},{4,36},{5,37},{6,38},{7,39},{8,40},{9,... | collective-permute-start | bytes 589832 | tf_op jit(solution)/shard_map/ppermute | solution.py:197
  56.9 15.5 %collective-permute-start.18 = (bf16[768,128]{1,0:T(8,128)(2,1)S(1)}, bf16[768,128]{1,0:T(8,128)(2,1)S(1)}, u32[]{:S(2)}, u32[]{:S(2)}) collective-permute-start(bf16[768,128]{1,0:T(8,128)(2,1)S(1)} %constant_dynamic-update-slice_fusion.6), channel_id=1, source_target_pairs={{0,64},{1,65},{2,66},{3,67},{4,68},{5,69},{6,70},{7,71},{8,72},{9,... | collective-permute-start | bytes 589832 | tf_op jit(solution)/shard_map/ppermute | solution.py:197
  63.8 8.5 %collective-permute-start.19 = (bf16[768,128]{1,0:T(8,128)(2,1)S(1)}, bf16[768,128]{1,0:T(8,128)(2,1)S(1)}, u32[]{:S(2)}, u32[]{:S(2)}) collective-permute-start(bf16[768,128]{1,0:T(8,128)(2,1)S(1)} %constant_dynamic-update-slice_fusion.6), channel_id=1, source_target_pairs={{0,96},{1,97},{2,98},{3,99},{4,100},{5,101},{6,102},{7,103},{8,104... | collective-permute-start | bytes 589832 | tf_op jit(solution)/shard_map/ppermute | solution.py:197
  63.8 10.0 %collective-permute-start.7 = (bf16[768,128]{1,0:T(8,128)(2,1)S(1)}, bf16[768,128]{1,0:T(8,128)(2,1)S(1)}, u32[]{:S(2)}, u32[]{:S(2)}) collective-permute-start(bf16[768,128]{1,0:T(8,128)(2,1)S(1)} %constant_dynamic-update-slice_fusion.2), channel_id=1, source_target_pairs={{0,8},{1,9},{2,10},{3,11},{4,12},{5,13},{6,14},{7,15},{8,16},{9,17... | collective-permute-start | bytes 589832 | tf_op jit(solution)/shard_map/ppermute | solution.py:197
  65.0 13.5 %collective-permute-start.8 = (bf16[768,128]{1,0:T(8,128)(2,1)S(1)}, bf16[768,128]{1,0:T(8,128)(2,1)S(1)}, u32[]{:S(2)}, u32[]{:S(2)}) collective-permute-start(bf16[768,128]{1,0:T(8,128)(2,1)S(1)} %constant_dynamic-update-slice_fusion.2), channel_id=1, source_target_pairs={{0,16},{1,17},{2,18},{3,19},{4,20},{5,21},{6,22},{7,23},{8,24},{9,... | collective-permute-start | bytes 589832 | tf_op jit(solution)/shard_map/ppermute | solution.py:197
  68.1 11.7 %collective-permute-start.9 = (bf16[768,128]{1,0:T(8,128)(2,1)S(1)}, bf16[768,128]{1,0:T(8,128)(2,1)S(1)}, u32[]{:S(2)}, u32[]{:S(2)}) collective-permute-start(bf16[768,128]{1,0:T(8,128)(2,1)S(1)} %constant_dynamic-update-slice_fusion.2), channel_id=1, source_target_pairs={{0,24},{1,25},{2,26},{3,27},{4,28},{5,29},{6,30},{7,31},{8,0},{9,1... | collective-permute-start | bytes 589832 | tf_op jit(solution)/shard_map/ppermute | solution.py:197
  72.4 11.0 %collective-permute-start.2 = (bf16[768,128]{1,0:T(8,128)(2,1)S(1)}, bf16[768,128]{1,0:T(8,128)(2,1)S(1)}, u32[]{:S(2)}, u32[]{:S(2)}) collective-permute-start(bf16[768,128]{1,0:T(8,128)(2,1)S(1)} %constant_dynamic-update-slice_fusion), channel_id=1, source_target_pairs={{0,8},{1,9},{2,10},{3,11},{4,12},{5,13},{6,14},{7,15},{8,16},{9,17... | collective-permute-start | bytes 589832 | tf_op jit(solution)/shard_map/ppermute | solution.py:197
  72.4 11.0 %collective-permute-start.3 = (bf16[768,128]{1,0:T(8,128)(2,1)S(1)}, bf16[768,128]{1,0:T(8,128)(2,1)S(1)}, u32[]{:S(2)}, u32[]{:S(2)}) collective-permute-start(bf16[768,128]{1,0:T(8,128)(2,1)S(1)} %constant_dynamic-update-slice_fusion), channel_id=1, source_target_pairs={{0,16},{1,17},{2,18},{3,19},{4,20},{5,21},{6,22},{7,23},{8,24},{9,... | collective-permute-start | bytes 589832 | tf_op jit(solution)/shard_map/ppermute | solution.py:197
  73.8 9.5 %collective-permute-start.4 = (bf16[768,128]{1,0:T(8,128)(2,1)S(1)}, bf16[768,128]{1,0:T(8,128)(2,1)S(1)}, u32[]{:S(2)}, u32[]{:S(2)}) collective-permute-start(bf16[768,128]{1,0:T(8,128)(2,1)S(1)} %constant_dynamic-update-slice_fusion), channel_id=1, source_target_pairs={{0,24},{1,25},{2,26},{3,27},{4,28},{5,29},{6,30},{7,31},{8,0},{9,1... | collective-permute-start | bytes 589832 | tf_op jit(solution)/shard_map/ppermute | solution.py:197
  217.3 11.5 %collective-permute-start.38 = (bf16[128,768]{1,0:T(8,128)(2,1)S(1)}, bf16[128,768]{1,0:T(8,128)(2,1)S(1)}, u32[]{:S(2)}, u32[]{:S(2)}) collective-permute-start(bf16[128,768]{1,0:T(8,128)(2,1)S(1)} %get-tuple-element.25), channel_id=1, source_target_pairs={{0,96},{1,97},{2,98},{3,99},{4,100},{5,101},{6,102},{7,103},{8,104... | collective-permute-start | bytes 589832 | tf_op jit(solution)/shard_map/ppermute | solution.py:197
  219.4 9.4 %collective-permute-start.39 = (bf16[128,768]{1,0:T(8,128)(2,1)S(1)}, bf16[128,768]{1,0:T(8,128)(2,1)S(1)}, u32[]{:S(2)}, u32[]{:S(2)}) collective-permute-start(bf16[128,768]{1,0:T(8,128)(2,1)S(1)} %get-tuple-element.27), channel_id=1, source_target_pairs={{0,64},{1,65},{2,66},{3,67},{4,68},{5,69},{6,70},{7,71},{8,72},{9,... | collective-permute-start | bytes 589832 | tf_op jit(solution)/shard_map/ppermute | solution.py:197
  220.3 12.7 %collective-permute-start.40 = (bf16[128,768]{1,0:T(8,128)(2,1)S(1)}, bf16[128,768]{1,0:T(8,128)(2,1)S(1)}, u32[]{:S(2)}, u32[]{:S(2)}) collective-permute-start(bf16[128,768]{1,0:T(8,128)(2,1)S(1)} %get-tuple-element.26), channel_id=1, source_target_pairs={{0,32},{1,33},{2,34},{3,35},{4,36},{5,37},{6,38},{7,39},{8,40},{9,... | collective-permute-start | bytes 589832 | tf_op jit(solution)/shard_map/ppermute | solution.py:197
  220.9 15.5 %collective-permute-start.33 = (bf16[128,768]{1,0:T(8,128)(2,1)S(1)}, bf16[128,768]{1,0:T(8,128)(2,1)S(1)}, u32[]{:S(2)}, u32[]{:S(2)}) collective-permute-start(bf16[128,768]{1,0:T(8,128)(2,1)S(1)} %get-tuple-element.28), channel_id=1, source_target_pairs={{0,96},{1,97},{2,98},{3,99},{4,100},{5,101},{6,102},{7,103},{8,104... | collective-permute-start | bytes 589832 | tf_op jit(solution)/shard_map/ppermute | solution.py:197
  223.7 14.5 %collective-permute-start.34 = (bf16[128,768]{1,0:T(8,128)(2,1)S(1)}, bf16[128,768]{1,0:T(8,128)(2,1)S(1)}, u32[]{:S(2)}, u32[]{:S(2)}) collective-permute-start(bf16[128,768]{1,0:T(8,128)(2,1)S(1)} %get-tuple-element.30), channel_id=1, source_target_pairs={{0,64},{1,65},{2,66},{3,67},{4,68},{5,69},{6,70},{7,71},{8,72},{9,... | collective-permute-start | bytes 589832 | tf_op jit(solution)/shard_map/ppermute | solution.py:197
  228.8 11.1 %collective-permute-start.35 = (bf16[128,768]{1,0:T(8,128)(2,1)S(1)}, bf16[128,768]{1,0:T(8,128)(2,1)S(1)}, u32[]{:S(2)}, u32[]{:S(2)}) collective-permute-start(bf16[128,768]{1,0:T(8,128)(2,1)S(1)} %get-tuple-element.29), channel_id=1, source_target_pairs={{0,32},{1,33},{2,34},{3,35},{4,36},{5,37},{6,38},{7,39},{8,40},{9,... | collective-permute-start | bytes 589832 | tf_op jit(solution)/shard_map/ppermute | solution.py:197
  228.8 12.8 %collective-permute-start.28 = (bf16[128,768]{1,0:T(8,128)(2,1)S(1)}, bf16[128,768]{1,0:T(8,128)(2,1)S(1)}, u32[]{:S(2)}, u32[]{:S(2)}) collective-permute-start(bf16[128,768]{1,0:T(8,128)(2,1)S(1)} %get-tuple-element.31), channel_id=1, source_target_pairs={{0,24},{1,25},{2,26},{3,27},{4,28},{5,29},{6,30},{7,31},{8,0},{9,1... | collective-permute-start | bytes 589832 | tf_op jit(solution)/shard_map/ppermute | solution.py:197
  233.0 9.6 %collective-permute-start.29 = (bf16[128,768]{1,0:T(8,128)(2,1)S(1)}, bf16[128,768]{1,0:T(8,128)(2,1)S(1)}, u32[]{:S(2)}, u32[]{:S(2)}) collective-permute-start(bf16[128,768]{1,0:T(8,128)(2,1)S(1)} %get-tuple-element.33), channel_id=1, source_target_pairs={{0,16},{1,17},{2,18},{3,19},{4,20},{5,21},{6,22},{7,23},{8,24},{9,... | collective-permute-start | bytes 589832 | tf_op jit(solution)/shard_map/ppermute | solution.py:197
  236.4 9.3 %collective-permute-start.30 = (bf16[128,768]{1,0:T(8,128)(2,1)S(1)}, bf16[128,768]{1,0:T(8,128)(2,1)S(1)}, u32[]{:S(2)}, u32[]{:S(2)}) collective-permute-start(bf16[128,768]{1,0:T(8,128)(2,1)S(1)} %get-tuple-element.32), channel_id=1, source_target_pairs={{0,8},{1,9},{2,10},{3,11},{4,12},{5,13},{6,14},{7,15},{8,16},{9,17... | collective-permute-start | bytes 589832 | tf_op jit(solution)/shard_map/ppermute | solution.py:197
  238.2 8.5 %collective-permute-start.41 = (bf16[128,384]{1,0:T(8,128)(2,1)S(1)}, bf16[128,384]{1,0:T(8,128)(2,1)S(1)}, u32[]{:S(2)}, u32[]{:S(2)}) collective-permute-start(bf16[128,384]{1,0:T(8,128)(2,1)S(1)} %get-tuple-element.36), channel_id=1, source_target_pairs={{0,2},{1,3},{2,0},{3,1},{4,6},{5,7},{6,4},{7,5},{8,10},{9,11},{10,... | collective-permute-start | bytes 294920 | tf_op jit(solution)/shard_map/ppermute | solution.py:197
  239.9 8.0 %collective-permute-start.42 = (bf16[128,384]{1,0:T(8,128)(2,1)S(1)}, bf16[128,384]{1,0:T(8,128)(2,1)S(1)}, u32[]{:S(2)}, u32[]{:S(2)}) collective-permute-start(bf16[128,384]{1,0:T(8,128)(2,1)S(1)} %get-tuple-element.37), channel_id=1, source_target_pairs={{0,6},{1,7},{2,4},{3,5},{4,2},{5,3},{6,0},{7,1},{8,14},{9,15},{10,... | collective-permute-start | bytes 294920 | tf_op jit(solution)/shard_map/ppermute | solution.py:197
  (22 other events, 179.2 us)
Sparse Core Ops, SparseCore 0:
  27.5 356.2 all-reduce.1

commit v2 on v1

v2 whole, which is shorter than its diff:
```python
import functools

import jax
import jax.numpy as jnp
from jax import lax
from jax.experimental import pallas as pl
from jax.experimental.pallas import tpu as pltpu
from jax.sharding import PartitionSpec as P

HEAD_DIM = 64
LOG2E = 1.4426950408889634
f32 = jnp.float32
bf16 = jnp.bfloat16
AXES = ("seq", "head")


def dot(a, b, dims=((1,), (0,))):
    return lax.dot_general(a, b, (dims, ((), ())), preferred_element_type=f32)


def split3(x):
    a = x.astype(bf16).astype(f32)
    r = x - a
    b = r.astype(bf16).astype(f32)
    return a, b, r - b


def prep_query(q, do, sm, aug, qa, doa, q_t, do_t):
    n = q.shape[0]
    rows = []
    for h in range(2):
        rows += list(split3(sm[h : h + 1, :] * (-8.0)))
    for h in range(2):
        rows += list(split3(-sm[2 + h : 3 + h, :]))
    c = [sm[4 + d : 5 + d, :] for d in range(3)]
    rows += c
    rows += list(split3(1.0 + (c[0] * c[0] + c[1] * c[1] + c[2] * c[2])))
    rows += [jnp.ones((1, n), f32)] * 3
    rows += [jnp.zeros((24 - len(rows), n), f32)]
    top = jnp.concatenate(rows, axis=0)
    fill = jnp.zeros((40, n), f32)
    a = jnp.concatenate([top, fill, top, fill], axis=0).T.astype(bf16)
    aug[...] = a
    low = lax.broadcasted_iota(jnp.int32, (n, 128), 1) < HEAD_DIM
    qa[0] = jnp.where(low, q, a)
    qa[1] = jnp.where(low, a, q)
    doa[0] = jnp.where(low, do, a)
    doa[1] = jnp.where(low, a, do)
    q_t[...] = q.T
    do_t[...] = do.T


def prep_key(k, v, cj, ka_t, va_t, ca_t, k_t):
    n = k.shape[0]
    kt = k.T
    vt = v.T
    k_t[...] = kt
    row = lax.broadcasted_iota(jnp.int32, (128, n), 0)
    low = row < HEAD_DIM
    pos = jnp.where(low, row, row - HEAD_DIM)

    def pick(start):
        hit = (pos >= start) & (pos < start + 3)
        return jnp.where(hit, 1.0, 0.0).astype(bf16)

    ka_t[0] = jnp.where(low, kt, pick(0))
    ka_t[1] = jnp.where(low, pick(3), kt)
    va_t[0] = jnp.where(low, vt, pick(6))
    va_t[1] = jnp.where(low, pick(9), vt)
    c = [cj[d : d + 1, :] for d in range(3)]
    m = split3(c[0] * c[0] + c[1] * c[1] + c[2] * c[2])
    ca = jnp.concatenate(
        [jnp.zeros((12, n), f32)]
        + [-2.0 * x for x in c]
        + [jnp.ones((3, n), f32)]
        + list(m)
        + [jnp.zeros((128 - 21, n), f32)],
        axis=0,
    )
    ca_t[...] = ca.astype(bf16)


def tile(qa, doa, aug, q_t, do_t, ka_t, va_t, ca_t, k_t, rates, dq_t, dk_t, dv_t, ds, i, j, bi, bj):
    ii = pl.ds(i, bi)
    jj = pl.ds(j, bj)
    l2 = jnp.maximum(dot(aug[ii, :], ca_t[:, jj]), 1.0)
    lengths = l2 * lax.rsqrt(l2)
    ps = []
    gs = []
    for h in range(2):
        s = dot(qa[h, ii, :], ka_t[h, :, jj])
        gp = dot(doa[h, ii, :], va_t[h, :, jj])
        p = jnp.exp2(s * (LOG2E / 8.0) - lengths * rates[h])
        g = p * gp
        ds[h] += jnp.sum((g * lengths).reshape(bi // 8, 8, bj), axis=0)
        ps.append(p.astype(bf16))
        gs.append(g.astype(bf16))
    for h in range(2):
        hh = pl.ds(h * HEAD_DIM, HEAD_DIM)
        dv_t[hh, jj] += dot(do_t[hh, ii], ps[h])
        dk_t[hh, jj] += dot(q_t[hh, ii], gs[h])
        dq_t[hh, ii] += dot(k_t[hh, jj], gs[h], ((1,), (1,)))


ORDER = [(q, k) for k in (1, 3, 2) for q in (0, 1, 3, 2)] + [(2, 0), (1, 0), (3, 0), (0, 0)]


def pick_at(t, values):
    out = jnp.int32(values[-1])
    for i in range(len(values) - 2, -1, -1):
        out = jnp.where(t <= i, jnp.int32(values[i]), out)
    return out


def place():
    seq = lax.axis_index("seq")
    head = lax.axis_index("head")
    return seq // 8, (seq // 2) % 4, seq % 2, head // 2, head % 2


def whole_kernel(
    query, key, value, attn_out, log_norm, d_output, out_weight, coords, slopes,
    d_query, d_key, d_value, d_weight, d_slopes,
    piece, qs, dos, sm, kv, cj, sm_src, pair_src, w_part, w_send, w_in, w_sum, w_z, w_x, w_all,
    aug, qa, doa, q_t, do_t, ka_t, va_t, ca_t, k_t, dq_t, dk_t, dv_t, ds,
    dq_send, dq_in, dkv_send, dkv_in, back_send, back_in, ds_send, ds_in,
    send_sem, recv_sem,
):
    rows = query.shape[0]
    n = 2 * rows
    y, z, xh, xl, c = place()
    head = xl * 2 + c

    def at(y, z, xh, xl, c):
        return ((y * 4 + z) * 2 + xh, xl * 2 + c)

    twin = at(y, z, xh, xl, 1 - c)
    near = at(y, z, xh, 1 - xl, c)
    far = at(y, z, 1 - xh, 1 - xl, c)
    across = at(y, z, 1 - xh, xl, c)

    def on_z(s):
        return at(y, (z + s) % 4, xh, xl, c)

    def on_y(s):
        return at((y + s) % 4, z, xh, xl, c)

    partners = [twin, near, far, across] + [on_z(s) for s in (1, 2, 3)] + [on_y(s) for s in (1, 2, 3)]
    barrier = pltpu.get_barrier_semaphore()
    for device in partners:
        pl.semaphore_signal(barrier, inc=1, device_id=device, device_id_type=pl.DeviceIdType.MESH)

    lane = lax.broadcasted_iota(jnp.int32, (1, rows), 1)
    pos = coords[...].astype(f32)
    for p in range(2):
        rate = jnp.where(lane < 128, slopes[2 * p], slopes[2 * p + 1])
        sm_src[p] = jnp.concatenate(
            [log_norm[2 * p : 2 * p + 2, :], jnp.zeros((2, rows), f32), pos, rate], axis=0
        )
    place_rows = jnp.concatenate([pos, jnp.zeros((5, rows), f32)], axis=0)
    cj[0, :, :rows] = place_rows
    cj[4, :, :rows] = place_rows
    piece[head] = d_output[...]
    pl.semaphore_wait(barrier, len(partners))

    count = [0]

    def link(src, dst, device):
        i = count[0]
        count[0] += 1
        return lambda: pltpu.make_async_remote_copy(
            src_ref=src,
            dst_ref=dst,
            send_sem=send_sem.at[i],
            recv_sem=recv_sem.at[i],
            device_id=device,
            device_id_type=pl.DeviceIdType.MESH,
        )

    def start(links):
        for one in links:
            one().start()

    def received(links):
        for one in links:
            one().wait_recv()

    first = pl.ds(0, rows)
    second = pl.ds(rows, rows)
    mine = pl.ds(pl.multiple_of(xh * 128, 128), 128)
    other = pl.ds(pl.multiple_of((1 - xh) * 128, 128), 128)

    own_out = [link(piece.at[head], piece.at[head], near), link(piece.at[head], piece.at[head], twin)]
    near_head = (1 - xl) * 2 + c
    forward = [link(piece.at[near_head], piece.at[near_head], twin)]
    cross_kv = []
    for i, array in enumerate((key, value)):
        cross_kv += [
            link(array.at[:, mine], kv.at[0, i, first], near),
            link(array.at[:, other], kv.at[0, i, second], far),
        ]
    cross_kv += [link(cj.at[4, :, first], cj.at[0, :, second], far)]
    cross_q = [
        link(query.at[:, mine], qs.at[0, first], near),
        link(query.at[:, other], qs.at[0, second], far),
    ]
    cross_do = [
        link(pair_src.at[xh], dos.at[0, first], near),
        link(pair_src.at[1 - xh], dos.at[0, second], far),
        link(sm_src.at[xh], sm.at[0, :, first], near),
        link(sm_src.at[1 - xh], sm.at[0, :, second], far),
    ]
    gather_kv = {
        s: [link(kv.at[0], kv.at[s], on_y(s)), link(cj.at[0], cj.at[s], on_y(s))] for s in (1, 3, 2)
    }
    gather_q = {s: [link(qs.at[0], qs.at[s], on_z(s))] for s in (1, 3, 2)}
    gather_do = {
        s: [link(dos.at[0], dos.at[s], on_z(s)), link(sm.at[0], sm.at[s], on_z(s))] for s in (1, 3, 2)
    }
    give_q = {s: [link(dq_send.at[s], dq_in.at[s], on_z(4 - s))] for s in (1, 3, 2)}
    give_kv = {s: [link(dkv_send.at[s], dkv_in.at[s], on_y(4 - s))] for s in (1, 3, 2)}
    w_rs_y = [link(w_send.at[(y + s) % 4], w_in.at[s], on_y(s)) for s in (1, 3, 2)]
    w_rs_z = [link(w_sum.at[(z + s) % 4], w_z.at[s], on_z(s)) for s in (1, 3, 2)]
    w_rs_x = [link(w_x.at[0], w_x.at[1], across)]
    w_ag_z = [link(w_all.at[y, z], w_all.at[y, z], on_z(s)) for s in (1, 3, 2)]
    w_ag_y = [link(w_all.at[y], w_all.at[y], on_y(s)) for s in (1, 3, 2)]
    back = [
        [
            link(back_send.at[i, :, first], back_in.at[i, xh], near),
            link(back_send.at[i, :, second], back_in.at[i, xh], far),
        ]
        for i in range(3)
    ]
    ds_z = [link(ds_send.at[0], ds_in.at[0, s], on_z(s)) for s in (1, 3, 2)]
    ds_y = [link(ds_send.at[1], ds_in.at[1, s], on_y(s)) for s in (1, 3, 2)]
    ds_x = [
        link(ds_send.at[2], ds_in.at[2, xh], near),
        link(ds_send.at[2], ds_in.at[2, xh], far),
    ]

    start(own_out)
    start(cross_kv)
    start(cross_q)
    dq_t[...] = jnp.zeros_like(dq_t)
    dk_t[...] = jnp.zeros_like(dk_t)
    dv_t[...] = jnp.zeros_like(dv_t)
    ds[...] = jnp.zeros_like(ds)
    received(own_out[:1])
    start(forward)
    received(own_out[1:])
    received(forward)
    total = jnp.zeros((rows, 256), f32)
    for g in range(4):
        total = total + dot(piece[g], out_weight[:, g * 256 : (g + 1) * 256], ((1,), (1,)))
    d_attn = total.astype(bf16)
    product = (d_attn.astype(f32) * attn_out[...].astype(f32)).T
    for p in range(2):
        pair_src[p] = d_attn[:, p * 128 : (p + 1) * 128]
        for h in range(2):
            r = (2 * p + h) * HEAD_DIM
            sm_src[p, 2 + h : 3 + h, :] = jnp.sum(product[r : r + HEAD_DIM], axis=0, keepdims=True)
    start(cross_do)
    received(cross_kv)
    for s in (1, 3, 2):
        start(gather_kv[s])
    received(cross_q)
    for s in (1, 3, 2):
        start(gather_q[s])
    a_t = attn_out[...].T
    for g in range(4):
        part = dot(a_t, piece[g])
        for i in range(4):
            w_part[i, :, g * 256 : (g + 1) * 256] = part[i * 64 : (i + 1) * 64]
    w_send[...] = w_part[...].astype(bf16).reshape(w_send.shape)
    received(cross_do)
    for s in (1, 3, 2):
        start(gather_do[s])

    def prepare_query(s):
        prep_query(
            qs[s], dos[s], sm[s], aug.at[s], qa.at[s], doa.at[s], q_t.at[s], do_t.at[s]
        )

    def prepare_key(s):
        prep_key(kv[s, 0], kv[s, 1], cj[s], ka_t.at[s], va_t.at[s], ca_t.at[s], k_t.at[s])

    prepare_query(0)
    prepare_key(0)
    rates = [
        jnp.concatenate([sm[0, 7:8, h * 128 : (h + 1) * 128]] * (n // 128), axis=1) * LOG2E
        for h in range(2)
    ]

    def take_key(s):
        received(gather_kv[s])
        prepare_key(s)

    def take_query(s):
        received(gather_q[s])
        received(gather_do[s])
        prepare_query(s)

    def send_kv(s):
        dkv_send[s, 0] = dk_t[s].astype(bf16)
        dkv_send[s, 1] = dv_t[s].astype(bf16)
        start(give_kv[s])

    def send_q(s):
        dq_send[s] = dq_t[s].astype(bf16)
        start(give_q[s])

    def weight_y():
        received(w_rs_y)
        total = w_part[y].reshape(w_sum.shape)
        for s in (1, 2, 3):
            total = total + w_in[s].astype(f32)
        w_sum[...] = total
        start(w_rs_z)

    def weight_z():
        received(w_rs_z)
        w_x[0] = w_sum[z] + w_z[1] + w_z[2] + w_z[3]
        start(w_rs_x)

    def weight_x():
        received(w_rs_x)
        w_all[y, z] = (w_x[0] + w_x[1]).astype(bf16)
        start(w_ag_z)

    def weight_gather():
        received(w_ag_z)
        start(w_ag_y)

    def weight_end():
        received(w_ag_y)
        d_weight[...] = w_all[...].astype(f32).reshape(d_weight.shape)

    def add_kv():
        for s in (1, 2, 3):
            received(give_kv[s])
            dk_t[0] += dkv_in[s, 0].astype(f32)
            dv_t[0] += dkv_in[s, 1].astype(f32)

    def add_q(s):
        received(give_q[s])
        dq_t[0] += dq_in[s].astype(f32)

    before = {
        0: [lambda: take_key(1)],
        1: [lambda: take_query(1)],
        2: [lambda: take_query(3)],
        3: [lambda: take_query(2)],
        4: [lambda: send_kv(1), lambda: take_key(3), lambda: start(w_rs_y)],
        6: [weight_y],
        8: [lambda: send_kv(3), lambda: take_key(2), weight_z],
        9: [weight_x],
        10: [weight_gather],
        12: [lambda: send_kv(2)],
        13: [lambda: send_q(2), weight_end],
        14: [lambda: send_q(1)],
        15: [lambda: send_q(3), add_kv, lambda: add_q(2)],
    }

    def block(t, _):
        for step, events in before.items():

            @pl.when(t == step)
            def _(events=events):
                for event in events:
                    event()

        si = pick_at(t, [q for q, _ in ORDER])
        sj = pick_at(t, [k for _, k in ORDER])
        tile(
            qa.at[si], doa.at[si], aug.at[si], q_t.at[si], do_t.at[si],
            ka_t.at[sj], va_t.at[sj], ca_t.at[sj], k_t.at[sj], rates,
            dq_t.at[si], dk_t.at[sj], dv_t.at[sj], ds, 0, 0, n, n,
        )
        return 0

    lax.fori_loop(0, len(ORDER), block, 0)

    rates_sum = [
        jnp.sum(jnp.sum(-ds[h], axis=0, keepdims=True), axis=1, keepdims=True) for h in range(2)
    ]
    ds_send[0] = jnp.concatenate(
        [jnp.broadcast_to(r, (1, 128)) for r in rates_sum] + [jnp.zeros((6, 128), f32)], axis=0
    )
    start(ds_z)
    back_send[2] = dv_t[0].astype(bf16)
    start(back[2])
    back_send[1] = (dk_t[0] * 0.125).astype(bf16)
    start(back[1])
    received(ds_z)
    ds_send[1] = ds_send[0] + ds_in[0, 1] + ds_in[0, 2] + ds_in[0, 3]
    start(ds_y)
    add_q(1)
    add_q(3)
    back_send[0] = (dq_t[0] * 0.125).astype(bf16)
    start(back[0])
    received(ds_y)
    ds_send[2] = ds_send[1] + ds_in[1, 1] + ds_in[1, 2] + ds_in[1, 3]
    start(ds_x)
    for i, out in ((2, d_value), (1, d_key), (0, d_query)):
        received(back[i])
        for p in range(2):
            out[:, p * 128 : (p + 1) * 128] = back_in[i, p].T
    received(ds_x)
    d_slopes[...] = jnp.concatenate([ds_in[2, 0, 0:2], ds_in[2, 1, 0:2]], axis=0)

    sent = [own_out, forward, cross_kv, cross_q, cross_do, w_rs_y, w_rs_z, w_rs_x, w_ag_z, w_ag_y]
    sent += [group[s] for group in (gather_kv, gather_q, gather_do, give_q, give_kv) for s in (1, 2, 3)]
    sent += back + [ds_z, ds_y, ds_x]
    for links in sent:
        for one in links:
            one().wait_send()


LINKS = 62


def per_device(query, key, value, attn_out, log_norm, d_output, out_weight, coords, slopes):
    rows, cols = query.shape
    n = 2 * rows
    vm = pl.BlockSpec(memory_space=pltpu.VMEM)
    quarter = out_weight.shape[0] // 4

    def wide(*lead):
        return pltpu.VMEM(lead + (n, 128), bf16)

    def tall(dtype, *lead):
        return pltpu.VMEM(lead + (128, n), dtype)

    width = out_weight.shape[1]
    scratch = [
        pltpu.VMEM((4, rows, cols), bf16),
        wide(4), wide(4),
        pltpu.VMEM((4, 8, n), f32),
        wide(4, 2),
        pltpu.VMEM((5, 8, n), f32),
        pltpu.VMEM((2, 8, rows), f32),
        pltpu.VMEM((2, rows, 128), bf16),
        pltpu.VMEM((4, quarter, width), f32),
        pltpu.VMEM((4, 4, quarter // 4, width), bf16),
        pltpu.VMEM((4, 4, quarter // 4, width), bf16),
        pltpu.VMEM((4, quarter // 4, width), f32),
        pltpu.VMEM((4, quarter // 4, width), f32),
        pltpu.VMEM((2, quarter // 4, width), f32),
        pltpu.VMEM((4, 4, quarter // 4, width), bf16),
        wide(4), wide(4, 2), wide(4, 2), tall(bf16, 4), tall(bf16, 4),
        tall(bf16, 4, 2), tall(bf16, 4, 2), tall(bf16, 4), tall(bf16, 4),
        tall(f32, 4), tall(f32, 4), tall(f32, 4), pltpu.VMEM((2, 8, n), f32),
        tall(bf16, 4), tall(bf16, 4),
        tall(bf16, 4, 2), tall(bf16, 4, 2),
        tall(bf16, 3), pltpu.VMEM((3, 2, 128, rows), bf16),
        pltpu.VMEM((3, 8, 128), f32), pltpu.VMEM((3, 4, 8, 128), f32),
        pltpu.SemaphoreType.DMA((LINKS,)), pltpu.SemaphoreType.DMA((LINKS,)),
    ]
    d_query, d_key, d_value, d_weight, d_slopes = pl.pallas_call(
        whole_kernel,
        out_shape=[jax.ShapeDtypeStruct((rows, cols), bf16)] * 3
        + [jax.ShapeDtypeStruct(out_weight.shape, f32), jax.ShapeDtypeStruct((4, 128), f32)],
        in_specs=[vm] * 8 + [pl.BlockSpec(memory_space=pltpu.SMEM)],
        out_specs=[vm] * 5,
        scratch_shapes=scratch,
        compiler_params=pltpu.CompilerParams(
            collective_id=0, has_side_effects=True, vmem_limit_bytes=60 << 20
        ),
        name="whole",
    )(query, key, value, attn_out, log_norm, d_output, out_weight, coords, slopes)
    return d_query, d_key, d_value, d_weight, d_slopes[:, 0]


def solution(mesh):
    placed = (
        P("seq", "head"),
        P("seq", "head"),
        P("seq", "head"),
        P("seq", "head"),
        P("head", "seq"),
        P("seq", "head"),
        P("head", None),
        P(None, "seq"),
        P("head"),
    )
    return jax.shard_map(
        per_device,
        mesh=mesh,
        in_specs=placed,
        out_specs=(
            P("seq", "head"),
            P("seq", "head"),
            P("seq", "head"),
            P("head", None),
            P("head"),
        ),
        check_vma=False,
    )
```

time: 393 us -> 124 us (0.32)
  waiting for transfers between devices: 155 us -> 0 us
  blocking collectives: 72.2 us -> 0 us
  starting transfers between devices: 62.2 us -> 0 us
  Pallas kernels: 66.1 us -> 115 us
  between operations: 14.5 us -> 0.65 us
  other arithmetic: 7.98 us -> 0 us
  local copies, waits for them, and re-layouts: 13.3 us -> 7.21 us
    psum x1 -> x0, waiting for transfers between devices: 130 us -> none  [per_device(): weight_sum = lax.psum(weight_part, 'seq')]
    psum x1 -> x0, blocking collectives: 63.2 us -> none  [per_device(): slope_sum = lax.psum(mine, AXES)]
    ppermute x43 -> x0, starting transfers between devices: 62.1 us -> none  [permute(): lax.ppermute(x, AXES, [(number(*d), number(*move(*d))) for d in devices()])]
    pallas_call x1, Pallas kernels: 66.1 us -> 115 us  [per_device(): pl.pallas_call(whole_kernel, out_shape=[jax.ShapeDtypeStruct((rows, cols)...]
    ppermute x43 -> x0, waiting for transfers between devices: 24.5 us -> none  [permute(): lax.ppermute(x, AXES, [(number(*d), number(*move(*d))) for d in devices()])]
    all_gather x1 -> x0, blocking collectives: 9.02 us -> none  [per_device(): piece = lax.all_gather(d_output, 'head', axis=1, tiled=True)]
    another operation x5 -> x0, other arithmetic: 4.63 us -> none  [spread(): return jnp.stack([x] + [shift(x, s) for s in (1, 2, 3)])]
    unnamed x38 -> x6, local copies, waits for them, and re-layouts: 8.23 us -> 5.82 us
  transfers between devices with their start and end apart: 44 -> 0, of which waited for: 13 -> 0; matrix products, arithmetic and copies ran while one was open for 4% -> 0% of each run, Pallas kernels for 17% -> 0%
where the time goes in v2:
time: 124 us; the launch traced here: 123 us
  Pallas kernels  115 us (93%)
  local copies, waits for them, and re-layouts  7.21 us (6%)
    pallas_call x1, Pallas kernels, per_device(): pl.pallas_call(whole_kernel, out_shape=[jax.ShapeDtypeStruct((rows, cols)...  115 us
    unnamed x6, local copies, waits for them, and re-layouts  5.82 us

profile of v2, /device:TPU:0, one launch (start us, length us, event | category | flops | bytes accessed | tf_op | source)
XLA Modules:
  0.0 123.2 jit_solution(2520308203945805451)
XLA Ops:
  0.6 115.3 %whole.1 = (bf16[384,256]{1,0:T(8,128)(2,1)}, bf16[384,256]{1,0:T(8,128)(2,1)}, bf16[384,256]{1,0:T(8,128)(2,1)}, f32[256,1024]{1,0:T(8,128)}, f32[4,128]{1,0:T(4,128)}) custom-call(bf16[384,256]{1,0:T(8,128)(2,1)} %query.1, bf16[384,256]{1,0:T(8,128)(2,1)} %key.1, bf16[384,256]{1,0:T(8,128)(2,1)} %value.1, bf16[384,256]{1,0:T(8,128)(2,1)} %attn_out.1, ...), custom_call_target="tpu_custom_call" | custom-call | tf_op jit(solution)/shard_map/whole/pallas_call | solution.py:459
  115.9 0.0 copy-start
  116.0 1.4 %slice_reduce_fusion = f32[4]{0:T(128)} fusion(f32[4,128]{1,0:T(4,128)} %get-tuple-element.14), kind=kLoop, calls=%fused_computation | loop fusion | bytes 32 | tf_op jit(solution)/shard_map/slice | solution.py:471
  117.3 1.6 %copy.18 = bf16[384,256]{1,0:T(8,128)(2,1)} copy(bf16[384,256]{1,0:T(8,128)(2,1)} %get-tuple-element.20) | data formatting | bytes 393216
  119.0 1.6 %copy.19 = bf16[384,256]{1,0:T(8,128)(2,1)} copy(bf16[384,256]{1,0:T(8,128)(2,1)} %get-tuple-element.21) | data formatting | bytes 393216
  120.6 1.6 %copy.20 = bf16[384,256]{1,0:T(8,128)(2,1)} copy(bf16[384,256]{1,0:T(8,128)(2,1)} %get-tuple-element.22) | data formatting | bytes 393216
  122.2 0.0 copy-done
  122.2 1.0 copy.21
Async XLA Ops:
  115.9 6.2 %copy-start = (f32[256,1024]{1,0:T(8,128)S(1)}, f32[256,1024]{1,0:T(8,128)}, u32[]{:S(2)}) copy-start(f32[256,1024]{1,0:T(8,128)} %get-tuple-element.23) | copy-start | bytes 3145732

commit v3 on v2

--- a/solution.py
+++ b/solution.py
@@ -80,29 +80,38 @@
     ca_t[...] = ca.astype(bf16)
 
 
-def tile(qa, doa, aug, q_t, do_t, ka_t, va_t, ca_t, k_t, rates, dq_t, dk_t, dv_t, ds, i, j, bi, bj):
-    ii = pl.ds(i, bi)
-    jj = pl.ds(j, bj)
-    l2 = jnp.maximum(dot(aug[ii, :], ca_t[:, jj]), 1.0)
-    lengths = l2 * lax.rsqrt(l2)
-    ps = []
-    gs = []
-    for h in range(2):
-        s = dot(qa[h, ii, :], ka_t[h, :, jj])
-        gp = dot(doa[h, ii, :], va_t[h, :, jj])
-        p = jnp.exp2(s * (LOG2E / 8.0) - lengths * rates[h])
-        g = p * gp
-        ds[h] += jnp.sum((g * lengths).reshape(bi // 8, 8, bj), axis=0)
-        ps.append(p.astype(bf16))
-        gs.append(g.astype(bf16))
-    for h in range(2):
+CHUNK = 256
+
+
+def tile(qa, doa, aug, q_t, do_t, ka_t, va_t, ca_t, k_t, rates, dq_t, dk_t, dv_t, ds):
+    n = q_t.shape[1]
+    pending = []
+
+    def gradients(h, ii, jj, p, g):
         hh = pl.ds(h * HEAD_DIM, HEAD_DIM)
-        dv_t[hh, jj] += dot(do_t[hh, ii], ps[h])
-        dk_t[hh, jj] += dot(q_t[hh, ii], gs[h])
-        dq_t[hh, ii] += dot(k_t[hh, jj], gs[h], ((1,), (1,)))
-
-
-ORDER = [(q, k) for k in (1, 3, 2) for q in (0, 1, 3, 2)] + [(2, 0), (1, 0), (3, 0), (0, 0)]
+        dv_t[hh, jj] += dot(do_t[hh, ii], p)
+        dk_t[hh, jj] += dot(q_t[hh, ii], g)
+        dq_t[hh, ii] += dot(k_t[hh, jj], g, ((1,), (1,)))
+
+    for i in range(0, n, CHUNK):
+        for j in range(0, n, CHUNK):
+            ii = pl.ds(i, CHUNK)
+            jj = pl.ds(j, CHUNK)
+            l2 = jnp.maximum(dot(aug[ii, :], ca_t[:, jj]), 1.0)
+            lengths = l2 * lax.rsqrt(l2)
+            for h in range(2):
+                s = dot(qa[h, ii, :], ka_t[h, :, jj])
+                gp = dot(doa[h, ii, :], va_t[h, :, jj])
+                p = jnp.exp2(s * (LOG2E / 8.0) - lengths * rates[h])
+                g = p * gp
+                ds[h] += jnp.sum((g * lengths).reshape(CHUNK // 8, 8, CHUNK), axis=0)
+                pending.append((h, ii, jj, p.astype(bf16), g.astype(bf16)))
+                if len(pending) > 1:
+                    gradients(*pending.pop(0))
+    gradients(*pending.pop(0))
+
+
+ORDER = [(0, 0)] + [(q, k) for k in (1, 2, 3) for q in (0, 1, 3, 2)] + [(2, 0), (1, 0), (3, 0)]
 
 
 def pick_at(t, values):
@@ -121,7 +130,7 @@
 def whole_kernel(
     query, key, value, attn_out, log_norm, d_output, out_weight, coords, slopes,
     d_query, d_key, d_value, d_weight, d_slopes,
-    piece, qs, dos, sm, kv, cj, sm_src, pair_src, w_part, w_send, w_in, w_sum, w_z, w_x, w_all,
+    a_in, o_w, local_sem, piece, qs, dos, sm, kv, cj, sm_src, pair_src, w_part, w_send, w_in, w_sum, w_y, w_x, w_all,
     aug, qa, doa, q_t, do_t, ka_t, va_t, ca_t, k_t, dq_t, dk_t, dv_t, ds,
     dq_send, dq_in, dkv_send, dkv_in, back_send, back_in, ds_send, ds_in,
     send_sem, recv_sem,
@@ -150,6 +159,14 @@
     for device in partners:
         pl.semaphore_signal(barrier, inc=1, device_id=device, device_id_type=pl.DeviceIdType.MESH)
 
+    local = [
+        pltpu.make_async_copy(src, dst, local_sem.at[i])
+        for i, (src, dst) in enumerate(
+            ((d_output, piece.at[head]), (out_weight, o_w), (attn_out, a_in))
+        )
+    ]
+    for one in local:
+        one.start()
     lane = lax.broadcasted_iota(jnp.int32, (1, rows), 1)
     pos = coords[...].astype(f32)
     for p in range(2):
@@ -160,7 +177,6 @@
     place_rows = jnp.concatenate([pos, jnp.zeros((5, rows), f32)], axis=0)
     cj[0, :, :rows] = place_rows
     cj[4, :, :rows] = place_rows
-    piece[head] = d_output[...]
     pl.semaphore_wait(barrier, len(partners))
 
     count = [0]
@@ -190,20 +206,18 @@
     mine = pl.ds(pl.multiple_of(xh * 128, 128), 128)
     other = pl.ds(pl.multiple_of((1 - xh) * 128, 128), 128)
 
-    own_out = [link(piece.at[head], piece.at[head], near), link(piece.at[head], piece.at[head], twin)]
+    own_out = [link(d_output, piece.at[head], near), link(d_output, piece.at[head], twin)]
     near_head = (1 - xl) * 2 + c
     forward = [link(piece.at[near_head], piece.at[near_head], twin)]
-    cross_kv = []
-    for i, array in enumerate((key, value)):
-        cross_kv += [
-            link(array.at[:, mine], kv.at[0, i, first], near),
-            link(array.at[:, other], kv.at[0, i, second], far),
-        ]
-    cross_kv += [link(cj.at[4, :, first], cj.at[0, :, second], far)]
-    cross_q = [
-        link(query.at[:, mine], qs.at[0, first], near),
-        link(query.at[:, other], qs.at[0, second], far),
-    ]
+    near_kv = [
+        link(array.at[:, mine], kv.at[0, i, first], near) for i, array in enumerate((key, value))
+    ]
+    far_kv = [
+        link(array.at[:, other], kv.at[0, i, second], far) for i, array in enumerate((key, value))
+    ]
+    far_kv += [link(cj.at[4, :, first], cj.at[0, :, second], far)]
+    near_q = [link(query.at[:, mine], qs.at[0, first], near)]
+    far_q = [link(query.at[:, other], qs.at[0, second], far)]
     cross_do = [
         link(pair_src.at[xh], dos.at[0, first], near),
         link(pair_src.at[1 - xh], dos.at[0, second], far),
@@ -211,19 +225,34 @@
         link(sm_src.at[1 - xh], sm.at[0, :, second], far),
     ]
     gather_kv = {
-        s: [link(kv.at[0], kv.at[s], on_y(s)), link(cj.at[0], cj.at[s], on_y(s))] for s in (1, 3, 2)
+        s: [link(kv.at[0], kv.at[s], on_y(s)), link(cj.at[0], cj.at[s], on_y(s))] for s in (1, 3)
     }
-    gather_q = {s: [link(qs.at[0], qs.at[s], on_z(s))] for s in (1, 3, 2)}
+    gather_q = {s: [link(qs.at[0], qs.at[s], on_z(s))] for s in (1, 3)}
     gather_do = {
-        s: [link(dos.at[0], dos.at[s], on_z(s)), link(sm.at[0], sm.at[s], on_z(s))] for s in (1, 3, 2)
+        s: [link(dos.at[0], dos.at[s], on_z(s)), link(sm.at[0], sm.at[s], on_z(s))] for s in (1, 3)
+    }
+    relay_kv = {
+        s: [
+            link(kv.at[s, :, half], kv.at[2, :, half], on_y(s)),
+            link(cj.at[s, :, half], cj.at[2, :, half], on_y(s)),
+        ]
+        for s, half in ((1, first), (3, second))
+    }
+    relay_q = {
+        s: [
+            link(qs.at[s, half], qs.at[2, half], on_z(s)),
+            link(dos.at[s, half], dos.at[2, half], on_z(s)),
+            link(sm.at[s, :, half], sm.at[2, :, half], on_z(s)),
+        ]
+        for s, half in ((1, first), (3, second))
     }
     give_q = {s: [link(dq_send.at[s], dq_in.at[s], on_z(4 - s))] for s in (1, 3, 2)}
     give_kv = {s: [link(dkv_send.at[s], dkv_in.at[s], on_y(4 - s))] for s in (1, 3, 2)}
-    w_rs_y = [link(w_send.at[(y + s) % 4], w_in.at[s], on_y(s)) for s in (1, 3, 2)]
-    w_rs_z = [link(w_sum.at[(z + s) % 4], w_z.at[s], on_z(s)) for s in (1, 3, 2)]
+    w_rs_z = [link(w_send.at[(z + s) % 4], w_in.at[s], on_z(s)) for s in (1, 3, 2)]
+    w_rs_y = [link(w_sum.at[(y + s) % 4], w_y.at[s], on_y(s)) for s in (1, 3, 2)]
     w_rs_x = [link(w_x.at[0], w_x.at[1], across)]
-    w_ag_z = [link(w_all.at[y, z], w_all.at[y, z], on_z(s)) for s in (1, 3, 2)]
-    w_ag_y = [link(w_all.at[y], w_all.at[y], on_y(s)) for s in (1, 3, 2)]
+    w_ag_y = [link(w_all.at[z, y], w_all.at[z, y], on_y(s)) for s in (1, 3, 2)]
+    w_ag_z = [link(w_all.at[z], w_all.at[z], on_z(s)) for s in (1, 3, 2)]
     back = [
         [
             link(back_send.at[i, :, first], back_in.at[i, xh], near),
@@ -238,42 +267,51 @@
         link(ds_send.at[2], ds_in.at[2, xh], far),
     ]
 
-    start(own_out)
-    start(cross_kv)
-    start(cross_q)
+    start(far_kv)
+    start(near_kv)
+    start(far_q)
+    start(own_out[1:])
+    for one in near_kv:
+        one().wait_send()
+    start(own_out[:1])
     dq_t[...] = jnp.zeros_like(dq_t)
     dk_t[...] = jnp.zeros_like(dk_t)
     dv_t[...] = jnp.zeros_like(dv_t)
     ds[...] = jnp.zeros_like(ds)
+    received(far_kv)
+    received(near_kv)
+    for s in (1, 3):
+        start(gather_kv[s])
     received(own_out[:1])
     start(forward)
+    start(near_q)
     received(own_out[1:])
     received(forward)
+    for one in local:
+        one.wait()
     total = jnp.zeros((rows, 256), f32)
     for g in range(4):
-        total = total + dot(piece[g], out_weight[:, g * 256 : (g + 1) * 256], ((1,), (1,)))
+        total = total + dot(piece[g], o_w[:, g * 256 : (g + 1) * 256], ((1,), (1,)))
     d_attn = total.astype(bf16)
-    product = (d_attn.astype(f32) * attn_out[...].astype(f32)).T
+    product = (d_attn.astype(f32) * a_in[...].astype(f32)).T
     for p in range(2):
         pair_src[p] = d_attn[:, p * 128 : (p + 1) * 128]
         for h in range(2):
             r = (2 * p + h) * HEAD_DIM
             sm_src[p, 2 + h : 3 + h, :] = jnp.sum(product[r : r + HEAD_DIM], axis=0, keepdims=True)
     start(cross_do)
-    received(cross_kv)
-    for s in (1, 3, 2):
-        start(gather_kv[s])
-    received(cross_q)
-    for s in (1, 3, 2):
+    received(far_q)
+    received(near_q)
+    for s in (1, 3):
         start(gather_q[s])
-    a_t = attn_out[...].T
+    a_t = a_in[...].T
     for g in range(4):
         part = dot(a_t, piece[g])
         for i in range(4):
             w_part[i, :, g * 256 : (g + 1) * 256] = part[i * 64 : (i + 1) * 64]
     w_send[...] = w_part[...].astype(bf16).reshape(w_send.shape)
     received(cross_do)
-    for s in (1, 3, 2):
+    for s in (1, 3):
         start(gather_do[s])
 
     def prepare_query(s):
@@ -285,20 +323,35 @@
         prep_key(kv[s, 0], kv[s, 1], cj[s], ka_t.at[s], va_t.at[s], ca_t.at[s], k_t.at[s])
 
     prepare_query(0)
-    prepare_key(0)
     rates = [
-        jnp.concatenate([sm[0, 7:8, h * 128 : (h + 1) * 128]] * (n // 128), axis=1) * LOG2E
+        jnp.concatenate([sm[0, 7:8, h * 128 : (h + 1) * 128]] * (CHUNK // 128), axis=1) * LOG2E
         for h in range(2)
     ]
 
     def take_key(s):
         received(gather_kv[s])
+        start(relay_kv[s])
         prepare_key(s)
 
     def take_query(s):
         received(gather_q[s])
         received(gather_do[s])
+        start(relay_q[s])
         prepare_query(s)
+
+    def relay_key():
+        received(gather_kv[3])
+        start(relay_kv[3])
+
+    def far_key():
+        received(relay_kv[1])
+        received(relay_kv[3])
+        prepare_key(2)
+
+    def far_query():
+        received(relay_q[1])
+        received(relay_q[3])
+        prepare_query(2)
 
     def send_kv(s):
         dkv_send[s, 0] = dk_t[s].astype(bf16)
@@ -309,31 +362,27 @@
         dq_send[s] = dq_t[s].astype(bf16)
         start(give_q[s])
 
-    def weight_y():
-        received(w_rs_y)
-        total = w_part[y].reshape(w_sum.shape)
+    def weight_z():
+        received(w_rs_z)
+        total = w_part[z].reshape(w_sum.shape)
         for s in (1, 2, 3):
             total = total + w_in[s].astype(f32)
         w_sum[...] = total
-        start(w_rs_z)
-
-    def weight_z():
-        received(w_rs_z)
-        w_x[0] = w_sum[z] + w_z[1] + w_z[2] + w_z[3]
+        start(w_rs_y)
+
+    def weight_y():
+        received(w_rs_y)
+        w_x[0] = w_sum[y] + w_y[1] + w_y[2] + w_y[3]
         start(w_rs_x)
 
     def weight_x():
         received(w_rs_x)
-        w_all[y, z] = (w_x[0] + w_x[1]).astype(bf16)
+        w_all[z, y] = (w_x[0] + w_x[1]).astype(bf16)
+        start(w_ag_y)
+
+    def weight_gather():
+        received(w_ag_y)
         start(w_ag_z)
-
-    def weight_gather():
-        received(w_ag_z)
-        start(w_ag_y)
-
-    def weight_end():
-        received(w_ag_y)
-        d_weight[...] = w_all[...].astype(f32).reshape(d_weight.shape)
 
     def add_kv():
         for s in (1, 2, 3):
@@ -345,40 +394,54 @@
         received(give_q[s])
         dq_t[0] += dq_in[s].astype(f32)
 
+    prepare_key(0)
     before = {
-        0: [lambda: take_key(1)],
-        1: [lambda: take_query(1)],
-        2: [lambda: take_query(3)],
-        3: [lambda: take_query(2)],
-        4: [lambda: send_kv(1), lambda: take_key(3), lambda: start(w_rs_y)],
-        6: [weight_y],
-        8: [lambda: send_kv(3), lambda: take_key(2), weight_z],
-        9: [weight_x],
-        10: [weight_gather],
-        12: [lambda: send_kv(2)],
-        13: [lambda: send_q(2), weight_end],
-        14: [lambda: send_q(1)],
-        15: [lambda: send_q(3), add_kv, lambda: add_q(2)],
+        1: [lambda: take_key(1)],
+        2: [relay_key, lambda: take_query(1)],
+        3: [lambda: take_query(3)],
+        4: [far_query, lambda: start(w_rs_z)],
+        5: [far_key, lambda: send_kv(1)],
+        7: [weight_z],
+        9: [lambda: prepare_key(3), weight_y, lambda: send_kv(2)],
+        11: [weight_x],
+        13: [lambda: send_kv(3), weight_gather],
+        14: [lambda: send_q(2)],
+        15: [lambda: send_q(1), add_kv],
     }
 
+    def run_events(t, low, high):
+        steps = [step for step in before if low <= step < high]
+        if high - low == 1:
+            for event in before[low]:
+                event()
+        elif steps:
+            middle = (low + high) // 2
+            left = any(step < middle for step in steps)
+            right = any(step >= middle for step in steps)
+            if left and right:
+                lax.cond(
+                    t < middle,
+                    lambda: run_events(t, low, middle),
+                    lambda: run_events(t, middle, high),
+                )
+            elif left:
+                pl.when(t < middle)(lambda: run_events(t, low, middle))
+            else:
+                pl.when(t >= middle)(lambda: run_events(t, middle, high))
+
     def block(t, _):
-        for step, events in before.items():
-
-            @pl.when(t == step)
-            def _(events=events):
-                for event in events:
-                    event()
-
+        run_events(t, 0, len(ORDER))
         si = pick_at(t, [q for q, _ in ORDER])
         sj = pick_at(t, [k for _, k in ORDER])
         tile(
             qa.at[si], doa.at[si], aug.at[si], q_t.at[si], do_t.at[si],
             ka_t.at[sj], va_t.at[sj], ca_t.at[sj], k_t.at[sj], rates,
-            dq_t.at[si], dk_t.at[sj], dv_t.at[sj], ds, 0, 0, n, n,
+            dq_t.at[si], dk_t.at[sj], dv_t.at[sj], ds,
         )
         return 0
 
     lax.fori_loop(0, len(ORDER), block, 0)
+    send_q(3)
 
     rates_sum = [
         jnp.sum(jnp.sum(-ds[h], axis=0, keepdims=True), axis=1, keepdims=True) for h in range(2)
@@ -394,6 +457,7 @@
     received(ds_z)
     ds_send[1] = ds_send[0] + ds_in[0, 1] + ds_in[0, 2] + ds_in[0, 3]
     start(ds_y)
+    add_q(2)
     add_q(1)
     add_q(3)
     back_send[0] = (dq_t[0] * 0.125).astype(bf16)
@@ -405,18 +469,32 @@
         received(back[i])
         for p in range(2):
             out[:, p * 128 : (p + 1) * 128] = back_in[i, p].T
+    received(w_ag_z)
+    d_weight[...] = w_all[...].reshape(d_weight.shape)
     received(ds_x)
     d_slopes[...] = jnp.concatenate([ds_in[2, 0, 0:2], ds_in[2, 1, 0:2]], axis=0)
 
-    sent = [own_out, forward, cross_kv, cross_q, cross_do, w_rs_y, w_rs_z, w_rs_x, w_ag_z, w_ag_y]
-    sent += [group[s] for group in (gather_kv, gather_q, gather_do, give_q, give_kv) for s in (1, 2, 3)]
+    sent = [own_out, forward, far_kv, far_q, near_q, cross_do]
+    sent += [w_rs_z, w_rs_y, w_rs_x, w_ag_y, w_ag_z]
+    sent += [group[s] for group in (give_q, give_kv) for s in (1, 2, 3)]
+    groups = (gather_kv, gather_q, gather_do, relay_kv, relay_q)
+    sent += [group[s] for group in groups for s in (1, 3)]
     sent += back + [ds_z, ds_y, ds_x]
     for links in sent:
         for one in links:
             one().wait_send()
 
 
-LINKS = 62
+LINKS = 67
+
+
+def hand_over(q, k, v, w, s, d_query, d_key, d_value, d_weight, d_slopes):
+    d_query[...] = q[...]
+    d_key[...] = k[...]
+    d_value[...] = v[...]
+    d_weight[...] = w[...].astype(f32)
+    for i in range(4):
+        d_slopes[i] = s[i, 0]
 
 
 def per_device(query, key, value, attn_out, log_norm, d_output, out_weight, coords, slopes):
@@ -433,6 +511,8 @@
 
     width = out_weight.shape[1]
     scratch = [
+        pltpu.VMEM((rows, cols), bf16), pltpu.VMEM(out_weight.shape, bf16),
+        pltpu.SemaphoreType.DMA((3,)),
         pltpu.VMEM((4, rows, cols), bf16),
         wide(4), wide(4),
         pltpu.VMEM((4, 8, n), f32),
@@ -449,18 +529,20 @@
         pltpu.VMEM((4, 4, quarter // 4, width), bf16),
         wide(4), wide(4, 2), wide(4, 2), tall(bf16, 4), tall(bf16, 4),
         tall(bf16, 4, 2), tall(bf16, 4, 2), tall(bf16, 4), tall(bf16, 4),
-        tall(f32, 4), tall(f32, 4), tall(f32, 4), pltpu.VMEM((2, 8, n), f32),
+        tall(f32, 4), tall(f32, 4), tall(f32, 4), pltpu.VMEM((2, 8, CHUNK), f32),
         tall(bf16, 4), tall(bf16, 4),
         tall(bf16, 4, 2), tall(bf16, 4, 2),
         tall(bf16, 3), pltpu.VMEM((3, 2, 128, rows), bf16),
         pltpu.VMEM((3, 8, 128), f32), pltpu.VMEM((3, 4, 8, 128), f32),
         pltpu.SemaphoreType.DMA((LINKS,)), pltpu.SemaphoreType.DMA((LINKS,)),
     ]
-    d_query, d_key, d_value, d_weight, d_slopes = pl.pallas_call(
+    hbm = pl.BlockSpec(memory_space=pl.ANY)
+    smem = pl.BlockSpec(memory_space=pltpu.SMEM)
+    results = pl.pallas_call(
         whole_kernel,
         out_shape=[jax.ShapeDtypeStruct((rows, cols), bf16)] * 3
-        + [jax.ShapeDtypeStruct(out_weight.shape, f32), jax.ShapeDtypeStruct((4, 128), f32)],
-        in_specs=[vm] * 8 + [pl.BlockSpec(memory_space=pltpu.SMEM)],
+        + [jax.ShapeDtypeStruct(out_weight.shape, bf16), jax.ShapeDtypeStruct((4, 128), f32)],
+        in_specs=[hbm] * 4 + [vm] + [hbm] * 2 + [vm, smem],
         out_specs=[vm] * 5,
         scratch_shapes=scratch,
         compiler_params=pltpu.CompilerParams(
@@ -468,7 +550,15 @@
         ),
         name="whole",
     )(query, key, value, attn_out, log_norm, d_output, out_weight, coords, slopes)
-    return d_query, d_key, d_value, d_weight, d_slopes[:, 0]
+    return pl.pallas_call(
+        hand_over,
+        out_shape=[jax.ShapeDtypeStruct((rows, cols), bf16)] * 3
+        + [jax.ShapeDtypeStruct(out_weight.shape, f32), jax.ShapeDtypeStruct(slopes.shape, f32)],
+        in_specs=[vm] * 4 + [smem],
+        out_specs=[vm] * 4 + [smem],
+        compiler_params=pltpu.CompilerParams(vmem_limit_bytes=16 << 20),
+        name="hand_over",
+    )(*results)
 
 
 def solution(mesh):

time: 124 us -> 104 us (0.84)
  Pallas kernels: 115 us -> 98.1 us
  local copies, waits for them, and re-layouts: 7.21 us -> 4.47 us
    pallas_call x1, Pallas kernels: 115 us -> 96.3 us  [per_device(): pl.pallas_call(whole_kernel, out_shape=[jax.ShapeDtypeStruct((rows, cols)...]
    pallas_call x0 -> x1, Pallas kernels: none -> 1.81 us  [per_device(): pl.pallas_call(hand_over, out_shape=[jax.ShapeDtypeStruct((rows, cols), b...]
    slice x1 -> x0, local copies, waits for them, and re-layouts: 1.39 us -> none  [per_device(): return (d_query, d_key, d_value, d_weight, d_slopes[:, 0])]
    unnamed x6 -> x10, local copies, waits for them, and re-layouts: 5.82 us -> 4.47 us
where the time goes in v3:
time: 104 us; the launch traced here: 103 us
  Pallas kernels  98.1 us (94%)
  local copies, waits for them, and re-layouts  4.47 us (4%)
    pallas_call x1, Pallas kernels, per_device(): pl.pallas_call(whole_kernel, out_shape=[jax.ShapeDtypeStruct((rows, cols)...  96.3 us
    unnamed x10, local copies, waits for them, and re-layouts  4.47 us

profile of v3, /device:TPU:0, one launch (start us, length us, event | category | flops | bytes accessed | tf_op | source)
XLA Modules:
  0.0 103.3 jit_solution(13663274568749500213)
XLA Ops:
  0.6 96.3 %whole.1 = (bf16[384,256]{1,0:T(8,128)(2,1)}, bf16[384,256]{1,0:T(8,128)(2,1)}, bf16[384,256]{1,0:T(8,128)(2,1)}, bf16[256,1024]{1,0:T(8,128)(2,1)}, f32[4,128]{1,0:T(4,128)}) custom-call(bf16[384,256]{1,0:T(8,128)(2,1)} %query.1, bf16[384,256]{1,0:T(8,128)(2,1)} %key.1, bf16[384,256]{1,0:T(8,128)(2,1)} %value.1, bf16[384,256]{1,0:T(8,128)(2,1)} %attn_out.1, ...), custom_call_target="tpu_custom_call" | custom-call | tf_op jit(solution)/shard_map/whole/pallas_call | solution.py:541
  97.0 0.0 copy-start.4
  97.0 0.6 copy-done.4
  97.6 0.0 copy-start
  97.6 1.0 %copy-done = bf16[256,1024]{1,0:T(8,128)(2,1)S(1)} copy-done((bf16[256,1024]{1,0:T(8,128)(2,1)S(1)}, bf16[256,1024]{1,0:T(8,128)(2,1)}, u32[]{:S(2)}) %copy-start) | copy-done | bytes 524312
  98.7 0.0 copy-start.1
  98.7 0.9 copy-done.1
  99.6 0.0 copy-start.2
  99.6 0.9 copy-done.2
  100.5 0.0 copy-start.3
  100.5 0.9 copy-done.3
  101.5 1.8 %hand_over.1 = (bf16[384,256]{1,0:T(8,128)(2,1)}, bf16[384,256]{1,0:T(8,128)(2,1)}, bf16[384,256]{1,0:T(8,128)(2,1)}, f32[256,1024]{1,0:T(8,128)}, f32[4]{0:T(128)}) custom-call(bf16[384,256]{1,0:T(8,128)(2,1)S(1)} %copy-done.1, bf16[384,256]{1,0:T(8,128)(2,1)S(1)} %copy-done.2, bf16[384,256]{1,0:T(8,128)(2,1)S(1)} %copy-done.3, ...), custom_call_target="tpu_custom_call" | custom-call | tf_op jit(solution)/shard_map/hand_over/pallas_call | solution.py:553
Async XLA Ops:
  97.0 0.7 copy-start.4
  97.6 1.0 %copy-start = (bf16[256,1024]{1,0:T(8,128)(2,1)S(1)}, bf16[256,1024]{1,0:T(8,128)(2,1)}, u32[]{:S(2)}) copy-start(bf16[256,1024]{1,0:T(8,128)(2,1)} %get-tuple-element.13.w) | copy-start | bytes 1572868
  98.7 0.9 copy-start.1
  99.6 0.9 copy-start.2
  100.5 0.9 copy-start.3

commit v4 on v3

--- a/solution.py
+++ b/solution.py
@@ -89,15 +89,15 @@
 
     def gradients(h, ii, jj, p, g):
         hh = pl.ds(h * HEAD_DIM, HEAD_DIM)
+        dq_t[hh, ii] += dot(k_t[hh, jj], g, ((1,), (1,)))
         dv_t[hh, jj] += dot(do_t[hh, ii], p)
         dk_t[hh, jj] += dot(q_t[hh, ii], g)
-        dq_t[hh, ii] += dot(k_t[hh, jj], g, ((1,), (1,)))
 
     for i in range(0, n, CHUNK):
         for j in range(0, n, CHUNK):
             ii = pl.ds(i, CHUNK)
             jj = pl.ds(j, CHUNK)
-            l2 = jnp.maximum(dot(aug[ii, :], ca_t[:, jj]), 1.0)
+            l2 = dot(aug[ii, :], ca_t[:, jj])
             lengths = l2 * lax.rsqrt(l2)
             for h in range(2):
                 s = dot(qa[h, ii, :], ka_t[h, :, jj])
@@ -111,7 +111,8 @@
     gradients(*pending.pop(0))
 
 
-ORDER = [(0, 0)] + [(q, k) for k in (1, 2, 3) for q in (0, 1, 3, 2)] + [(2, 0), (1, 0), (3, 0)]
+ORDER = [(0, 0), (0, 1), (0, 3), (1, 1), (3, 1), (2, 1)]
+ORDER += [(0, 2), (1, 2), (3, 2), (2, 2), (1, 3), (3, 3), (2, 3), (2, 0), (1, 0), (3, 0)]
 
 
 def pick_at(t, values):
@@ -130,7 +131,7 @@
 def whole_kernel(
     query, key, value, attn_out, log_norm, d_output, out_weight, coords, slopes,
     d_query, d_key, d_value, d_weight, d_slopes,
-    a_in, o_w, local_sem, piece, qs, dos, sm, kv, cj, sm_src, pair_src, w_part, w_send, w_in, w_sum, w_y, w_x, w_all,
+    a_in, o_w, local_sem, piece, qs, dos, sm, kv, cj, sm_src, pair_src, w_part, w_send, w_x, w_sum, w_send_y, w_y, w_sum_y, w_z, w_all,
     aug, qa, doa, q_t, do_t, ka_t, va_t, ca_t, k_t, dq_t, dk_t, dv_t, ds,
     dq_send, dq_in, dkv_send, dkv_in, back_send, back_in, ds_send, ds_in,
     send_sem, recv_sem,
@@ -248,11 +249,12 @@
     }
     give_q = {s: [link(dq_send.at[s], dq_in.at[s], on_z(4 - s))] for s in (1, 3, 2)}
     give_kv = {s: [link(dkv_send.at[s], dkv_in.at[s], on_y(4 - s))] for s in (1, 3, 2)}
-    w_rs_z = [link(w_send.at[(z + s) % 4], w_in.at[s], on_z(s)) for s in (1, 3, 2)]
-    w_rs_y = [link(w_sum.at[(y + s) % 4], w_y.at[s], on_y(s)) for s in (1, 3, 2)]
-    w_rs_x = [link(w_x.at[0], w_x.at[1], across)]
-    w_ag_y = [link(w_all.at[z, y], w_all.at[z, y], on_y(s)) for s in (1, 3, 2)]
-    w_ag_z = [link(w_all.at[z], w_all.at[z], on_z(s)) for s in (1, 3, 2)]
+    w_rs_x = [link(w_send, w_x, across)]
+    w_rs_y = [link(w_send_y.at[(y + s) % 4], w_y.at[s], on_y(s)) for s in (1, 3, 2)]
+    w_rs_z = [link(w_sum_y.at[(z + s) % 4], w_z.at[s], on_z(s)) for s in (1, 3, 2)]
+    w_ag_z = [link(w_all.at[xh, y, z], w_all.at[xh, y, z], on_z(s)) for s in (1, 3, 2)]
+    w_ag_y = [link(w_all.at[xh, y], w_all.at[xh, y], on_y(s)) for s in (1, 3, 2)]
+    w_ag_x = [link(w_all.at[xh], w_all.at[xh], across)]
     back = [
         [
             link(back_send.at[i, :, first], back_in.at[i, xh], near),
@@ -307,12 +309,12 @@
     a_t = a_in[...].T
     for g in range(4):
         part = dot(a_t, piece[g])
-        for i in range(4):
-            w_part[i, :, g * 256 : (g + 1) * 256] = part[i * 64 : (i + 1) * 64]
-    w_send[...] = w_part[...].astype(bf16).reshape(w_send.shape)
+        w_part[g // 2, :, :, :, (g % 2) * 256 : (g % 2 + 1) * 256] = part.reshape(4, 4, 16, 256)
+    w_send[...] = w_part[1 - xh].astype(bf16)
     received(cross_do)
     for s in (1, 3):
         start(gather_do[s])
+    start(w_rs_x)
 
     def prepare_query(s):
         prep_query(
@@ -333,15 +335,12 @@
         start(relay_kv[s])
         prepare_key(s)
 
-    def take_query(s):
-        received(gather_q[s])
-        received(gather_do[s])
-        start(relay_q[s])
-        prepare_query(s)
-
-    def relay_key():
-        received(gather_kv[3])
-        start(relay_kv[3])
+    def take_queries():
+        for s in (1, 3):
+            received(gather_q[s])
+            received(gather_do[s])
+            start(relay_q[s])
+        prepare_query(1)
 
     def far_key():
         received(relay_kv[1])
@@ -362,33 +361,37 @@
         dq_send[s] = dq_t[s].astype(bf16)
         start(give_q[s])
 
+    def weight_x():
+        received(w_rs_x)
+        w_sum[...] = w_part[xh] + w_x[...].astype(f32)
+        w_send_y[...] = w_sum[...].astype(bf16)
+        start(w_rs_y)
+
+    def weight_y():
+        received(w_rs_y)
+        total = w_sum[y]
+        for s in (1, 2, 3):
+            total = total + w_y[s].astype(f32)
+        w_sum_y[...] = total
+        start(w_rs_z)
+
     def weight_z():
         received(w_rs_z)
-        total = w_part[z].reshape(w_sum.shape)
-        for s in (1, 2, 3):
-            total = total + w_in[s].astype(f32)
-        w_sum[...] = total
-        start(w_rs_y)
-
-    def weight_y():
-        received(w_rs_y)
-        w_x[0] = w_sum[y] + w_y[1] + w_y[2] + w_y[3]
-        start(w_rs_x)
-
-    def weight_x():
-        received(w_rs_x)
-        w_all[z, y] = (w_x[0] + w_x[1]).astype(bf16)
+        w_all[xh, y, z] = (w_sum_y[z] + w_z[1] + w_z[2] + w_z[3]).astype(bf16)
+        start(w_ag_z)
+
+    def weight_gather_y():
+        received(w_ag_z)
         start(w_ag_y)
 
-    def weight_gather():
+    def weight_gather_x():
         received(w_ag_y)
-        start(w_ag_z)
-
-    def add_kv():
-        for s in (1, 2, 3):
-            received(give_kv[s])
-            dk_t[0] += dkv_in[s, 0].astype(f32)
-            dv_t[0] += dkv_in[s, 1].astype(f32)
+        start(w_ag_x)
+
+    def add_kv(s):
+        received(give_kv[s])
+        dk_t[0] += dkv_in[s, 0].astype(f32)
+        dv_t[0] += dkv_in[s, 1].astype(f32)
 
     def add_q(s):
         received(give_q[s])
@@ -397,16 +400,17 @@
     prepare_key(0)
     before = {
         1: [lambda: take_key(1)],
-        2: [relay_key, lambda: take_query(1)],
-        3: [lambda: take_query(3)],
-        4: [far_query, lambda: start(w_rs_z)],
-        5: [far_key, lambda: send_kv(1)],
-        7: [weight_z],
-        9: [lambda: prepare_key(3), weight_y, lambda: send_kv(2)],
-        11: [weight_x],
-        13: [lambda: send_kv(3), weight_gather],
+        2: [lambda: take_key(3)],
+        3: [take_queries],
+        4: [weight_x, lambda: prepare_query(3)],
+        5: [far_query],
+        6: [weight_y, lambda: send_kv(1), far_key],
+        8: [weight_z],
+        10: [weight_gather_y, lambda: send_kv(2)],
+        12: [weight_gather_x],
+        13: [lambda: send_kv(3)],
         14: [lambda: send_q(2)],
-        15: [lambda: send_q(1), add_kv],
+        15: [lambda: send_q(1), lambda: add_kv(1), lambda: add_kv(2)],
     }
 
     def run_events(t, low, high):
@@ -450,6 +454,7 @@
         [jnp.broadcast_to(r, (1, 128)) for r in rates_sum] + [jnp.zeros((6, 128), f32)], axis=0
     )
     start(ds_z)
+    add_kv(3)
     back_send[2] = dv_t[0].astype(bf16)
     start(back[2])
     back_send[1] = (dk_t[0] * 0.125).astype(bf16)
@@ -459,23 +464,24 @@
     start(ds_y)
     add_q(2)
     add_q(1)
+    received(ds_y)
+    ds_send[2] = ds_send[1] + ds_in[1, 1] + ds_in[1, 2] + ds_in[1, 3]
+    start(ds_x)
     add_q(3)
     back_send[0] = (dq_t[0] * 0.125).astype(bf16)
     start(back[0])
-    received(ds_y)
-    ds_send[2] = ds_send[1] + ds_in[1, 1] + ds_in[1, 2] + ds_in[1, 3]
-    start(ds_x)
     for i, out in ((2, d_value), (1, d_key), (0, d_query)):
         received(back[i])
         for p in range(2):
             out[:, p * 128 : (p + 1) * 128] = back_in[i, p].T
-    received(w_ag_z)
-    d_weight[...] = w_all[...].reshape(d_weight.shape)
+    received(w_ag_x)
+    for i in range(2):
+        d_weight[:, i * 512 : (i + 1) * 512] = w_all[i].reshape(256, 512)
     received(ds_x)
     d_slopes[...] = jnp.concatenate([ds_in[2, 0, 0:2], ds_in[2, 1, 0:2]], axis=0)
 
     sent = [own_out, forward, far_kv, far_q, near_q, cross_do]
-    sent += [w_rs_z, w_rs_y, w_rs_x, w_ag_y, w_ag_z]
+    sent += [w_rs_x, w_rs_z, w_rs_y, w_ag_y, w_ag_z, w_ag_x]
     sent += [group[s] for group in (give_q, give_kv) for s in (1, 2, 3)]
     groups = (gather_kv, gather_q, gather_do, relay_kv, relay_q)
     sent += [group[s] for group in groups for s in (1, 3)]
@@ -485,7 +491,7 @@
             one().wait_send()
 
 
-LINKS = 67
+LINKS = 68
 
 
 def hand_over(q, k, v, w, s, d_query, d_key, d_value, d_weight, d_slopes):
@@ -501,7 +507,7 @@
     rows, cols = query.shape
     n = 2 * rows
     vm = pl.BlockSpec(memory_space=pltpu.VMEM)
-    quarter = out_weight.shape[0] // 4
+    part = (4, 4, out_weight.shape[0] // 16, out_weight.shape[1] // 2)
 
     def wide(*lead):
         return pltpu.VMEM(lead + (n, 128), bf16)
@@ -509,7 +515,6 @@
     def tall(dtype, *lead):
         return pltpu.VMEM(lead + (128, n), dtype)
 
-    width = out_weight.shape[1]
     scratch = [
         pltpu.VMEM((rows, cols), bf16), pltpu.VMEM(out_weight.shape, bf16),
         pltpu.SemaphoreType.DMA((3,)),
@@ -520,13 +525,12 @@
         pltpu.VMEM((5, 8, n), f32),
         pltpu.VMEM((2, 8, rows), f32),
         pltpu.VMEM((2, rows, 128), bf16),
-        pltpu.VMEM((4, quarter, width), f32),
-        pltpu.VMEM((4, 4, quarter // 4, width), bf16),
-        pltpu.VMEM((4, 4, quarter // 4, width), bf16),
-        pltpu.VMEM((4, quarter // 4, width), f32),
-        pltpu.VMEM((4, quarter // 4, width), f32),
-        pltpu.VMEM((2, quarter // 4, width), f32),
-        pltpu.VMEM((4, 4, quarter // 4, width), bf16),
+        pltpu.VMEM((2,) + part, f32),
+        pltpu.VMEM(part, bf16), pltpu.VMEM(part, bf16),
+        pltpu.VMEM(part, f32),
+        pltpu.VMEM(part, bf16), pltpu.VMEM(part, bf16),
+        pltpu.VMEM(part[1:], f32), pltpu.VMEM(part[1:], f32),
+        pltpu.VMEM((2,) + part, bf16),
         wide(4), wide(4, 2), wide(4, 2), tall(bf16, 4), tall(bf16, 4),
         tall(bf16, 4, 2), tall(bf16, 4, 2), tall(bf16, 4), tall(bf16, 4),
         tall(f32, 4), tall(f32, 4), tall(f32, 4), pltpu.VMEM((2, 8, CHUNK), f32),
@@ -556,7 +560,7 @@
         + [jax.ShapeDtypeStruct(out_weight.shape, f32), jax.ShapeDtypeStruct(slopes.shape, f32)],
         in_specs=[vm] * 4 + [smem],
         out_specs=[vm] * 4 + [smem],
-        compiler_params=pltpu.CompilerParams(vmem_limit_bytes=16 << 20),
+        compiler_params=pltpu.CompilerParams(vmem_limit_bytes=60 << 20),
         name="hand_over",
     )(*results)
 

time: 104 us -> 94.3 us (0.907)
  Pallas kernels: 98.1 us -> 93.5 us
  local copies, waits for them, and re-layouts: 4.47 us -> 0 us
    pallas_call x1, Pallas kernels: 96.3 us -> 91 us  [per_device(): pl.pallas_call(whole_kernel, out_shape=[jax.ShapeDtypeStruct((rows, cols)...]
    unnamed x10 -> x0, local copies, waits for them, and re-layouts: 4.47 us -> none
where the time goes in v4:
time: 94.3 us; the launch traced here: 94.2 us
  Pallas kernels  93.5 us (99%)
    pallas_call x1, Pallas kernels, per_device(): pl.pallas_call(whole_kernel, out_shape=[jax.ShapeDtypeStruct((rows, cols)...  91 us
    pallas_call x1, Pallas kernels, per_device(): pl.pallas_call(hand_over, out_shape=[jax.ShapeDtypeStruct((rows, cols), b...  2.54 us

profile of v4, /device:TPU:0, one launch (start us, length us, event | category | flops | bytes accessed | tf_op | source)
XLA Modules:
  0.0 94.2 jit_solution(5848205105135332701)
XLA Ops:
  0.6 91.0 %whole.1 = (bf16[384,256]{1,0:T(8,128)(2,1)}, bf16[384,256]{1,0:T(8,128)(2,1)}, bf16[384,256]{1,0:T(8,128)(2,1)}, bf16[256,1024]{1,0:T(8,128)(2,1)}, f32[4,128]{1,0:T(4,128)}) custom-call(bf16[384,256]{1,0:T(8,128)(2,1)} %query.1, bf16[384,256]{1,0:T(8,128)(2,1)} %key.1, bf16[384,256]{1,0:T(8,128)(2,1)} %value.1, bf16[384,256]{1,0:T(8,128)(2,1)} %attn_out.1, ...), custom_call_target="tpu_custom_call" | custom-call | tf_op jit(solution)/shard_map/whole/pallas_call | solution.py:545
  91.6 2.5 %hand_over.1 = (bf16[384,256]{1,0:T(8,128)(2,1)}, bf16[384,256]{1,0:T(8,128)(2,1)}, bf16[384,256]{1,0:T(8,128)(2,1)}, f32[256,1024]{1,0:T(8,128)}, f32[4]{0:T(128)}) custom-call(bf16[384,256]{1,0:T(8,128)(2,1)} %get-tuple-element.10.q, bf16[384,256]{1,0:T(8,128)(2,1)} %get-tuple-element.11.k, bf16[384,256]{1,0:T(8,128)(2,1)} %get-tuple-element.12.v, ...), custom_call_target="tpu_custom_call" | custom-call | tf_op jit(solution)/shard_map/hand_over/pallas_call | solution.py:557

commit v5 on v4

--- a/solution.py
+++ b/solution.py
@@ -83,36 +83,40 @@
 CHUNK = 256
 
 
-def tile(qa, doa, aug, q_t, do_t, ka_t, va_t, ca_t, k_t, rates, dq_t, dk_t, dv_t, ds):
-    n = q_t.shape[1]
+def tile(parts, ka_t, va_t, ca_t, k_t, dk_t, dv_t, rates, ds):
+    n = k_t.shape[1]
     pending = []
 
-    def gradients(h, ii, jj, p, g):
+    def gradients(part, h, ii, jj, p, g):
+        _, _, _, q_t, do_t, dq_t = part
         hh = pl.ds(h * HEAD_DIM, HEAD_DIM)
         dq_t[hh, ii] += dot(k_t[hh, jj], g, ((1,), (1,)))
         dv_t[hh, jj] += dot(do_t[hh, ii], p)
         dk_t[hh, jj] += dot(q_t[hh, ii], g)
 
-    for i in range(0, n, CHUNK):
-        for j in range(0, n, CHUNK):
-            ii = pl.ds(i, CHUNK)
-            jj = pl.ds(j, CHUNK)
-            l2 = dot(aug[ii, :], ca_t[:, jj])
-            lengths = l2 * lax.rsqrt(l2)
-            for h in range(2):
-                s = dot(qa[h, ii, :], ka_t[h, :, jj])
-                gp = dot(doa[h, ii, :], va_t[h, :, jj])
-                p = jnp.exp2(s * (LOG2E / 8.0) - lengths * rates[h])
-                g = p * gp
-                ds[h] += jnp.sum((g * lengths).reshape(CHUNK // 8, 8, CHUNK), axis=0)
-                pending.append((h, ii, jj, p.astype(bf16), g.astype(bf16)))
-                if len(pending) > 1:
-                    gradients(*pending.pop(0))
+    for part in parts:
+        qa, doa, aug = part[:3]
+        for i in range(0, n, CHUNK):
+            for j in range(0, n, CHUNK):
+                ii = pl.ds(i, CHUNK)
+                jj = pl.ds(j, CHUNK)
+                l2 = dot(aug[ii, :], ca_t[:, jj])
+                lengths = l2 * lax.rsqrt(l2)
+                for h in range(2):
+                    s = dot(qa[h, ii, :], ka_t[h, :, jj])
+                    gp = dot(doa[h, ii, :], va_t[h, :, jj])
+                    p = jnp.exp2(s * (LOG2E / 8.0) - lengths * rates[h])
+                    g = p * gp
+                    ds[h] += jnp.sum((g * lengths).reshape(CHUNK // 8, 8, CHUNK), axis=0)
+                    pending.append((part, h, ii, jj, p.astype(bf16), g.astype(bf16)))
+                    if len(pending) > 1:
+                        gradients(*pending.pop(0))
     gradients(*pending.pop(0))
 
 
-ORDER = [(0, 0), (0, 1), (0, 3), (1, 1), (3, 1), (2, 1)]
-ORDER += [(0, 2), (1, 2), (3, 2), (2, 2), (1, 3), (3, 3), (2, 3), (2, 0), (1, 0), (3, 0)]
+START = [((q,), k) for q, k in ((0, 0), (0, 1), (0, 3), (1, 1), (3, 1), (2, 1))]
+PAIRS = [((0, 1), 2), ((3, 2), 2), ((1, 3), 3)]
+END = [((q,), k) for q, k in ((2, 3), (2, 0), (1, 0), (3, 0))]
 
 
 def pick_at(t, values):
@@ -413,38 +417,41 @@
         15: [lambda: send_q(1), lambda: add_kv(1), lambda: add_kv(2)],
     }
 
-    def run_events(t, low, high):
-        steps = [step for step in before if low <= step < high]
-        if high - low == 1:
-            for event in before[low]:
+    def run_events(t, steps):
+        if len(steps) == 1:
+            for event in before.get(steps[0], []):
                 event()
-        elif steps:
-            middle = (low + high) // 2
-            left = any(step < middle for step in steps)
-            right = any(step >= middle for step in steps)
-            if left and right:
-                lax.cond(
-                    t < middle,
-                    lambda: run_events(t, low, middle),
-                    lambda: run_events(t, middle, high),
-                )
-            elif left:
-                pl.when(t < middle)(lambda: run_events(t, low, middle))
-            else:
-                pl.when(t >= middle)(lambda: run_events(t, middle, high))
-
-    def block(t, _):
-        run_events(t, 0, len(ORDER))
-        si = pick_at(t, [q for q, _ in ORDER])
-        sj = pick_at(t, [k for _, k in ORDER])
-        tile(
-            qa.at[si], doa.at[si], aug.at[si], q_t.at[si], do_t.at[si],
-            ka_t.at[sj], va_t.at[sj], ca_t.at[sj], k_t.at[sj], rates,
-            dq_t.at[si], dk_t.at[sj], dv_t.at[sj], ds,
-        )
-        return 0
-
-    lax.fori_loop(0, len(ORDER), block, 0)
+        else:
+            middle = len(steps) // 2
+            lax.cond(
+                t < steps[middle],
+                lambda: run_events(t, steps[:middle]),
+                lambda: run_events(t, steps[middle:]),
+            )
+
+    def blocks(order, first_step):
+        width = len(order[0][0])
+        steps = [first_step + i * width for i in range(len(order))]
+
+        def block(i, _):
+            run_events(first_step + i * width, steps)
+            sj = pick_at(i, [k for _, k in order])
+            parts = []
+            for m in range(width):
+                si = pick_at(i, [q[m] for q, _ in order])
+                parts.append([x.at[si] for x in (qa, doa, aug, q_t, do_t, dq_t)])
+            tile(
+                parts, ka_t.at[sj], va_t.at[sj], ca_t.at[sj], k_t.at[sj], dk_t.at[sj], dv_t.at[sj],
+                rates, ds,
+            )
+            return 0
+
+        lax.fori_loop(0, len(order), block, 0)
+        return first_step + len(order) * width
+
+    step = blocks(START, 0)
+    step = blocks(PAIRS, step)
+    blocks(END, step)
     send_q(3)
 
     rates_sum = [

time: 94.3 us -> 93.4 us (level)
  Pallas kernels: 93.5 us -> 92.4 us
    pallas_call x1, Pallas kernels: 91 us -> 89.9 us  [per_device(): pl.pallas_call(whole_kernel, out_shape=[jax.ShapeDtypeStruct((rows, cols)...]
where the time goes in v5:
time: 93.4 us; the launch traced here: 93.2 us
  Pallas kernels  92.4 us (99%)
    pallas_call x1, Pallas kernels, per_device(): pl.pallas_call(whole_kernel, out_shape=[jax.ShapeDtypeStruct((rows, cols)...  89.9 us
    pallas_call x1, Pallas kernels, per_device(): pl.pallas_call(hand_over, out_shape=[jax.ShapeDtypeStruct((rows, cols), b...  2.54 us

profile of v5, /device:TPU:0, one launch (start us, length us, event | category | flops | bytes accessed | tf_op | source)
XLA Modules:
  0.0 93.2 jit_solution(2903310917044210637)
XLA Ops:
  0.6 89.9 %whole.1 = (bf16[384,256]{1,0:T(8,128)(2,1)}, bf16[384,256]{1,0:T(8,128)(2,1)}, bf16[384,256]{1,0:T(8,128)(2,1)}, bf16[256,1024]{1,0:T(8,128)(2,1)}, f32[4,128]{1,0:T(4,128)}) custom-call(bf16[384,256]{1,0:T(8,128)(2,1)} %query.1, bf16[384,256]{1,0:T(8,128)(2,1)} %key.1, bf16[384,256]{1,0:T(8,128)(2,1)} %value.1, bf16[384,256]{1,0:T(8,128)(2,1)} %attn_out.1, ...), custom_call_target="tpu_custom_call" | custom-call | tf_op jit(solution)/shard_map/whole/pallas_call | solution.py:552
  90.5 2.5 %hand_over.1 = (bf16[384,256]{1,0:T(8,128)(2,1)}, bf16[384,256]{1,0:T(8,128)(2,1)}, bf16[384,256]{1,0:T(8,128)(2,1)}, f32[256,1024]{1,0:T(8,128)}, f32[4]{0:T(128)}) custom-call(bf16[384,256]{1,0:T(8,128)(2,1)} %get-tuple-element.10.q, bf16[384,256]{1,0:T(8,128)(2,1)} %get-tuple-element.11.k, bf16[384,256]{1,0:T(8,128)(2,1)} %get-tuple-element.12.v, ...), custom_call_target="tpu_custom_call" | custom-call | tf_op jit(solution)/shard_map/hand_over/pallas_call | solution.py:564

commit v6 on v5

--- a/solution.py
+++ b/solution.py
@@ -288,6 +288,10 @@
     received(near_kv)
     for s in (1, 3):
         start(gather_kv[s])
+    def prepare_key(s):
+        prep_key(kv[s, 0], kv[s, 1], cj[s], ka_t.at[s], va_t.at[s], ca_t.at[s], k_t.at[s])
+
+    prepare_key(0)
     received(own_out[:1])
     start(forward)
     start(near_q)
@@ -325,9 +329,6 @@
             qs[s], dos[s], sm[s], aug.at[s], qa.at[s], doa.at[s], q_t.at[s], do_t.at[s]
         )
 
-    def prepare_key(s):
-        prep_key(kv[s, 0], kv[s, 1], cj[s], ka_t.at[s], va_t.at[s], ca_t.at[s], k_t.at[s])
-
     prepare_query(0)
     rates = [
         jnp.concatenate([sm[0, 7:8, h * 128 : (h + 1) * 128]] * (CHUNK // 128), axis=1) * LOG2E
@@ -401,7 +402,6 @@
         received(give_q[s])
         dq_t[0] += dq_in[s].astype(f32)
 
-    prepare_key(0)
     before = {
         1: [lambda: take_key(1)],
         2: [lambda: take_key(3)],

time: 93.4 us -> 93.3 us (level)
  no operation moved by 1% of the time
where the time goes in v6:
time: 93.3 us; the launch traced here: 93.1 us
  Pallas kernels  92.3 us (99%)
    pallas_call x1, Pallas kernels, per_device(): pl.pallas_call(whole_kernel, out_shape=[jax.ShapeDtypeStruct((rows, cols)...  89.7 us
    pallas_call x1, Pallas kernels, per_device(): pl.pallas_call(hand_over, out_shape=[jax.ShapeDtypeStruct((rows, cols), b...  2.54 us

profile of v6, /device:TPU:0, one launch (start us, length us, event | category | flops | bytes accessed | tf_op | source)
XLA Modules:
  0.0 93.1 jit_solution(3281836221993110283)
XLA Ops:
  0.6 89.7 %whole.1 = (bf16[384,256]{1,0:T(8,128)(2,1)}, bf16[384,256]{1,0:T(8,128)(2,1)}, bf16[384,256]{1,0:T(8,128)(2,1)}, bf16[256,1024]{1,0:T(8,128)(2,1)}, f32[4,128]{1,0:T(4,128)}) custom-call(bf16[384,256]{1,0:T(8,128)(2,1)} %query.1, bf16[384,256]{1,0:T(8,128)(2,1)} %key.1, bf16[384,256]{1,0:T(8,128)(2,1)} %value.1, bf16[384,256]{1,0:T(8,128)(2,1)} %attn_out.1, ...), custom_call_target="tpu_custom_call" | custom-call | tf_op jit(solution)/shard_map/whole/pallas_call | solution.py:552
  90.4 2.5 %hand_over.1 = (bf16[384,256]{1,0:T(8,128)(2,1)}, bf16[384,256]{1,0:T(8,128)(2,1)}, bf16[384,256]{1,0:T(8,128)(2,1)}, f32[256,1024]{1,0:T(8,128)}, f32[4]{0:T(128)}) custom-call(bf16[384,256]{1,0:T(8,128)(2,1)} %get-tuple-element.10.q, bf16[384,256]{1,0:T(8,128)(2,1)} %get-tuple-element.11.k, bf16[384,256]{1,0:T(8,128)(2,1)} %get-tuple-element.12.v, ...), custom_call_target="tpu_custom_call" | custom-call | tf_op jit(solution)/shard_map/hand_over/pallas_call | solution.py:564
